TPU v7x, 128 devices: a whole 4x4x4 slice. The times are simulated.
128 devices in a mesh: row: 8 (over x, z_lo), col: 16 (over z_hi, y, core).
Axes of the slice: x: 4, y: 4, z: 4 (z_hi: 2, z_lo: 2; z = z_hi * 2 + z_lo), core: 2. Of those that a mesh axis runs over, the one named last changes fastest.
Arguments:
- inputs: bfloat16 [1024, 8192], P('row', 'col'), may hold values from -6 to 6
- gate_weight: bfloat16 [8192, 16384], P('col', 'row'), may hold values from -0.0625 to 0.0625
- up_weight: bfloat16 [8192, 16384], P('col', 'row'), may hold values from -0.0625 to 0.0625
- down_weight: bfloat16 [16384, 8192], P('row', 'col'), may hold values from -0.046875 to 0.046875
- out_grad: bfloat16 [1024, 8192], P('row', 'col'), may hold values from -1.5 to 1.5
Outputs:
- mixed: bfloat16 [1024, 8192], P('row', 'col')
- grad_input: bfloat16 [1024, 8192], P('row', 'col')
- grad_gate: float32 [8192, 16384], P('col', 'row')
- grad_up: float32 [8192, 16384], P('col', 'row')
- grad_down: float32 [16384, 8192], P('row', 'col')
All inputs are finite; a program needn't handle non-finite values.
Results may differ from a plain program's by a relative error of at most 0.033.
Values may be sent and summed in bfloat16 or wider, within the bound.
A program may use at most 128 MiB of HBM per device.

v0:
```python
import jax
import jax.numpy as jnp
from jax import lax
from jax.sharding import PartitionSpec as P


def silu_parts(gate):
    sig = jax.nn.sigmoid(gate)
    return (gate * sig, sig * (1.0 + gate * (1.0 - sig)))


def contract_first(left, right):
    return lax.dot_general(
        left, right, (((0,), (0,)), ((), ())), preferred_element_type=jnp.float32
    )


def contract_last(left, right):
    return lax.dot_general(
        left, right, (((1,), (1,)), ((), ())), preferred_element_type=jnp.float32
    )


def body(inputs, gate_weight, up_weight, down_weight, out_grad):
    full_x = lax.all_gather(inputs, "row", axis=0, tiled=True)
    part_gate = jnp.dot(full_x, gate_weight, preferred_element_type=jnp.float32)
    part_up = jnp.dot(full_x, up_weight, preferred_element_type=jnp.float32)
    gate, up = (
        lax.psum_scatter(
            part_gate.astype(jnp.bfloat16), "col", scatter_dimension=0, tiled=True
        ).astype(jnp.float32),
        lax.psum_scatter(
            part_up.astype(jnp.bfloat16), "col", scatter_dimension=0, tiled=True
        ).astype(jnp.float32),
    )
    act, slope = silu_parts(gate)
    hidden = (act * up).astype(jnp.bfloat16)
    full_hidden = lax.all_gather(hidden, "col", axis=0, tiled=True)
    mixed = lax.psum_scatter(
        jnp.dot(full_hidden, down_weight, preferred_element_type=jnp.float32).astype(jnp.bfloat16),
        "row",
        scatter_dimension=0,
        tiled=True,
    )
    full_grad = lax.all_gather(out_grad, "row", axis=0, tiled=True)
    grad_down = contract_first(full_hidden, full_grad)
    part_act_grad = contract_last(full_grad, down_weight)
    act_grad = lax.psum_scatter(
        part_act_grad.astype(jnp.bfloat16), "col", scatter_dimension=0, tiled=True
    ).astype(jnp.float32)
    gate_share = (act_grad * up * slope).astype(jnp.bfloat16)
    up_share = (act_grad * act).astype(jnp.bfloat16)
    full_gate_grad, full_up_grad = (
        lax.all_gather(gate_share, "col", axis=0, tiled=True),
        lax.all_gather(up_share, "col", axis=0, tiled=True),
    )
    grad_gate = contract_first(full_x, full_gate_grad)
    grad_up = contract_first(full_x, full_up_grad)
    grad_input = lax.psum_scatter(
        (
            contract_last(full_gate_grad, gate_weight) + contract_last(full_up_grad, up_weight)
        ).astype(jnp.bfloat16),
        "row",
        scatter_dimension=0,
        tiled=True,
    )
    return (mixed, grad_input, grad_gate, grad_up, grad_down)


def solution(mesh):
    in_specs = (P("row", "col"), P("col", "row"), P("col", "row"), P("row", "col"), P("row", "col"))
    out_specs = (
        P("row", "col"),
        P("row", "col"),
        P("col", "row"),
        P("col", "row"),
        P("row", "col"),
    )
    return jax.shard_map(body, mesh=mesh, in_specs=in_specs, out_specs=out_specs, check_vma=False)
```

profile of v0, /device:TPU:1, one launch (start us, length us, event | category | flops | bytes accessed | tf_op | source)
XLA Modules:
  0.0 602.9 jit_solution(17806541074869529313)
XLA Ops:
  8.7 38.9 %all-gather.6.cloned.1.call-done = bf16[1024,512]{1,0:T(8,128)(2,1)} async-done(((bf16[128,512]{1,0:T(8,128)(2,1)}), bf16[1024,512]{1,0:T(8,128)(2,1)}) %all-gather.6.cloned.1.call-update) | async-done | bytes 1048592 | tf_op jit(solution)/shard_map/all_gather | solution.py:25
  47.6 5.6 convolution_convert_fusion.2
  53.2 1.1 copy-done.1
  54.4 5.9 convolution_convert_fusion.1
  60.4 27.7 %all-gather.10.cloned.1.call-done = bf16[1024,512]{1,0:T(8,128)(2,1)} async-done(((bf16[128,512]{1,0:T(8,128)(2,1)}), bf16[1024,512]{1,0:T(8,128)(2,1)}) %all-gather.10.cloned.1.call-update) | async-done | bytes 1048592 | tf_op jit(solution)/shard_map/all_gather | solution.py:45
  88.1 6.3 %convolution_convert_fusion = bf16[1024,2048]{1,0:T(8,128)(2,1)} fusion(bf16[1024,512]{1,0:T(8,128)(2,1)} %all-gather.10.cloned.1.call-done, bf16[2048,512]{1,0:T(8,128)(2,1)} %param.8), kind=kOutput, calls=%fused_computation | convolution fusion | flops 2149580800 | bytes 7340032 | tf_op jit(solution)/shard_map/dot_general | solution.py:19
  94.5 81.3 %reduce-scatter.6.cloned.1.call-done = bf16[64,2048]{1,0:T(8,128)(2,1)} async-done(((bf16[1024,2048]{1,0:T(8,128)(2,1)}), bf16[64,2048]{1,0:T(8,128)(2,1)}) %reduce-scatter.6.cloned.1.call-update) | async-done | bytes 262160 | tf_op jit(solution)/shard_map/reduce_scatter | solution.py:29
  175.8 84.0 %reduce-scatter.8.cloned.1.call-done = bf16[64,2048]{1,0:T(8,128)(2,1)} async-done(((bf16[1024,2048]{1,0:T(8,128)(2,1)}), bf16[64,2048]{1,0:T(8,128)(2,1)}) %reduce-scatter.8.cloned.1.call-update) | async-done | bytes 262160 | tf_op jit(solution)/shard_map/reduce_scatter | solution.py:32
  259.8 83.5 %reduce-scatter.12.cloned.1.call-done = bf16[64,2048]{1,0:T(8,128)(2,1)} async-done(((bf16[1024,2048]{1,0:T(8,128)(2,1)}), bf16[64,2048]{1,0:T(8,128)(2,1)}) %reduce-scatter.12.cloned.1.call-update) | async-done | bytes 262160 | tf_op jit(solution)/shard_map/reduce_scatter | solution.py:48
  343.2 2.3 fusion.3
  345.6 0.7 all-gather.14.cloned.1.call-update
  346.3 0.7 all-gather.8.cloned.1.call-update
  347.1 55.8 %all-gather.12.cloned.1.call-done = bf16[1024,2048]{1,0:T(8,128)(2,1)} async-done(((bf16[64,2048]{1,0:T(8,128)(2,1)}), bf16[1024,2048]{1,0:T(8,128)(2,1)}) %all-gather.12.cloned.1.call-update) | async-done | bytes 4194320 | tf_op jit(solution)/shard_map/all_gather | solution.py:54
  402.8 5.9 fusion.9
  408.7 52.2 %all-gather.14.cloned.1.call-done = bf16[1024,2048]{1,0:T(8,128)(2,1)} async-done(((bf16[64,2048]{1,0:T(8,128)(2,1)}), bf16[1024,2048]{1,0:T(8,128)(2,1)}) %all-gather.14.cloned.1.call-update) | async-done | bytes 4194320 | tf_op jit(solution)/shard_map/all_gather | solution.py:55
  460.9 6.8 %add_convert_fusion = bf16[1024,512]{1,0:T(8,128)(2,1)} fusion(f32[1024,512]{1,0:T(8,128)} %fusion.9, bf16[1024,2048]{1,0:T(8,128)(2,1)} %all-gather.14.cloned.1.call-done, bf16[512,2048]{1,0:T(8,128)(2,1)} %param.7), kind=kOutput, calls=%fused_computation.5 | convolution fusion | flops 2148532224 | bytes 9437184 | tf_op jit(solution)/shard_map/dot_general | solution.py:19
  467.9 51.0 %all-gather.8.cloned.1.call-done = bf16[1024,2048]{1,0:T(8,128)(2,1)} async-done(((bf16[64,2048]{1,0:T(8,128)(2,1)}), bf16[1024,2048]{1,0:T(8,128)(2,1)}) %all-gather.8.cloned.1.call-update) | async-done | bytes 4194320 | tf_op jit(solution)/shard_map/all_gather | solution.py:38
  519.0 6.2 %convolution_convert_fusion.3 = bf16[1024,512]{1,0:T(8,128)(2,1)} fusion(bf16[1024,2048]{1,0:T(8,128)(2,1)} %all-gather.8.cloned.1.call-done, bf16[2048,512]{1,0:T(8,128)(2,1)} %param.8), kind=kOutput, calls=%fused_computation.6 | convolution fusion | flops 2148007936 | bytes 7340032 | tf_op jit(solution)/shard_map/dot_general | solution.py:40
  525.1 6.6 %convolution_bitcast_fusion.1 = f32[512,2048]{0,1:T(8,128)} fusion(bf16[1024,2048]{1,0:T(8,128)(2,1)} %all-gather.12.cloned.1.call-done, bf16[1024,512]{1,0:T(8,128)(2,1)S(1)} %copy-done.1), kind=kOutput, calls=%fused_computation.4 | convolution fusion | flops 2147483648 | bytes 9437184 | tf_op jit(solution)/shard_map/dot_general | solution.py:13
  531.7 5.4 copy.10
  537.1 6.6 %convolution_bitcast_fusion = f32[512,2048]{0,1:T(8,128)} fusion(bf16[1024,2048]{1,0:T(8,128)(2,1)} %all-gather.14.cloned.1.call-done, bf16[1024,512]{1,0:T(8,128)(2,1)S(1)} %copy-done.1), kind=kOutput, calls=%fused_computation.3 | convolution fusion | flops 2147483648 | bytes 9437184 | tf_op jit(solution)/shard_map/dot_general | solution.py:13
  543.7 5.5 copy.11
  549.2 6.6 %fusion.10 = f32[2048,512]{1,0:T(8,128)} fusion(bf16[1024,2048]{1,0:T(8,128)(2,1)} %all-gather.8.cloned.1.call-done, bf16[1024,512]{1,0:T(8,128)(2,1)S(1)} %copy-done.2), kind=kOutput, calls=%fused_computation.23 | convolution fusion | flops 2147483648 | bytes 9437184 | tf_op jit(solution)/shard_map/dot_general | solution.py:13
  555.8 40.3 %reduce-scatter.10.cloned.1.call-done = bf16[128,512]{1,0:T(8,128)(2,1)} async-done(((bf16[1024,512]{1,0:T(8,128)(2,1)}), bf16[128,512]{1,0:T(8,128)(2,1)}) %reduce-scatter.10.cloned.1.call-update) | async-done | bytes 131088 | tf_op jit(solution)/shard_map/reduce_scatter | solution.py:39
  (24 shorter events, 2.1 us)
Async XLA Ops:
  7.2 40.4 %copy-start = (bf16[512,2048]{1,0:T(8,128)(2,1)S(1)}, bf16[512,2048]{1,0:T(8,128)(2,1)}, u32[]{:S(2)}) copy-start(bf16[512,2048]{1,0:T(8,128)(2,1)} %param.6) | copy-start | bytes 6291460
  7.2 40.4 %all-gather.6.cloned.1.call-start = ((), (), s32[]{:S(2)}) async-start(), calls=%async_computation.5 | async-start | bytes 1179648 | tf_op jit(solution)/shard_map/all_gather | solution.py:25
  7.9 80.2 %all-gather.10.cloned.1.call-start = ((), (), s32[]{:S(2)}) async-start(), calls=%async_computation.10 | async-start | bytes 1179648 | tf_op jit(solution)/shard_map/all_gather | solution.py:45
  8.7 167.1 %reduce-scatter.6.cloned.1.call-start = ((), (), s32[]{:S(2)}) async-start(), calls=%async_computation.6 | async-start | bytes 4456448 | tf_op jit(solution)/shard_map/reduce_scatter | solution.py:29
  53.2 1.2 copy-start.1
  53.2 206.6 %reduce-scatter.8.cloned.1.call-start = ((), (), s32[]{:S(2)}) async-start(), calls=%async_computation.7 | async-start | bytes 4456448 | tf_op jit(solution)/shard_map/reduce_scatter | solution.py:32
  60.3 282.9 %reduce-scatter.12.cloned.1.call-start = ((), (), s32[]{:S(2)}) async-start(), calls=%async_computation.11 | async-start | bytes 4456448 | tf_op jit(solution)/shard_map/reduce_scatter | solution.py:48
  94.5 308.4 %all-gather.12.cloned.1.call-start = ((), (), s32[]{:S(2)}) async-start(), calls=%async_computation.12 | async-start | bytes 4456448 | tf_op jit(solution)/shard_map/all_gather | solution.py:54
  345.5 115.4 %all-gather.14.cloned.1.call-start = ((), (), s32[]{:S(2)}) async-start(), calls=%async_computation.13 | async-start | bytes 4456448 | tf_op jit(solution)/shard_map/all_gather | solution.py:55
  346.3 172.7 %all-gather.8.cloned.1.call-start = ((), (), s32[]{:S(2)}) async-start(), calls=%async_computation.8 | async-start | bytes 4456448 | tf_op jit(solution)/shard_map/all_gather | solution.py:38
  347.0 208.7 %reduce-scatter.14.cloned.1.call-start = ((), (), s32[]{:S(2)}) async-start(), calls=%async_computation.14 | async-start | bytes 1179648 | tf_op jit(solution)/shard_map/reduce_scatter | solution.py:59
  467.7 128.4 %reduce-scatter.10.cloned.1.call-start = ((), (), s32[]{:S(2)}) async-start(), calls=%async_computation.9 | async-start | bytes 1179648 | tf_op jit(solution)/shard_map/reduce_scatter | solution.py:39
  543.7 5.5 copy-start.2
Sparse Core Ops, SparseCore 0:
  9.7 37.8 all-gather.5
  49.2 38.8 all-gather.9
  92.8 82.9 reduce-scatter.5
  180.8 78.9 reduce-scatter.7
  264.2 78.9 reduce-scatter.11
  346.4 56.3 all-gather.11
  406.2 54.7 all-gather.13
  464.2 54.7 all-gather.7
  522.1 32.9 reduce-scatter.13
  558.0 37.9 reduce-scatter.9
where the time goes:
time: 608 us; the launch traced here: 603 us
  waiting for transfers between devices  517 us (85%)
  matrix products  56.4 us (9%)
  between operations  14.2 us (2%)
  local copies, waits for them, and re-layouts  12 us (2%)
    reduce_scatter x1, waiting for transfers between devices, body(): lax.psum_scatter(part_up.astype(jnp.bfloat16), 'col', scatter_dimension=0...  84 us
    reduce_scatter x1, waiting for transfers between devices, body(): lax.psum_scatter(part_act_grad.astype(jnp.bfloat16), 'col', scatter_dimen...  83.5 us
    reduce_scatter x1, waiting for transfers between devices, body(): lax.psum_scatter(part_gate.astype(jnp.bfloat16), 'col', scatter_dimension...  81.3 us
    all_gather x1, waiting for transfers between devices, body(): lax.all_gather(gate_share, 'col', axis=0, tiled=True)  55.8 us
    all_gather x1, waiting for transfers between devices, body(): lax.all_gather(up_share, 'col', axis=0, tiled=True)  52.2 us
    all_gather x1, waiting for transfers between devices, body(): full_hidden = lax.all_gather(hidden, 'col', axis=0, tiled=True)  51 us
    reduce_scatter x1, waiting for transfers between devices, body(): lax.psum_scatter(jnp.dot(full_hidden, down_weight, preferred_element_type...  40.3 us
    all_gather x1, waiting for transfers between devices, body(): full_x = lax.all_gather(inputs, 'row', axis=0, tiled=True)  38.9 us
  transfers between devices with their start and end apart: 10, of which 9 were waited for; matrix products, arithmetic and copies ran while one was open for 11% of the time, Pallas kernels for 0%

commit v1 on v0

v1 whole, which is shorter than its diff:
```python
import functools

import jax
import jax.numpy as jnp
from jax import lax
from jax.experimental import pallas as pl
from jax.experimental.pallas import tpu as pltpu
from jax.sharding import PartitionSpec as P

MESH = pl.DeviceIdType.MESH
BF16, F32 = jnp.bfloat16, jnp.float32
CHUNKS = 4
NN = (((1,), (0,)), ((), ()))
NT = (((1,), (1,)), ((), ()))
TN = (((0,), (0,)), ((), ()))


def dot(left, right, dims):
    return lax.dot_general(left, right, dims, preferred_element_type=F32)


def silu_parts(gate):
    sig = jax.nn.sigmoid(gate)
    return gate * sig, sig * (1.0 + gate * (1.0 - sig))


def kernel(
    x_hbm, og_hbm, wg_hbm, wu_hbm, wd_hbm,
    h_out, gg_out, ug_out, xf_out, of_out, mix_out, gi_out,
    xo, wg, wu, wd, part, core_in, y1b, y2b, zb, za, y1a, y2a, full, mix, mix_x, mix_z, outs,
    send_sem, recv_sem, load_sem, weight_sem, store_sem, out_sem,
):
    row, col = lax.axis_index("row"), lax.axis_index("col")
    x, zl = row // 2, row % 2
    zh, y, core = col // 8, (col // 2) % 4, col % 2
    zo, other = 1 - zh, 1 - core
    y_next, y_prev, y_far = (y + 1) % 4, (y + 3) % 4, (y + 2) % 4
    rows, width = x_hbm.shape
    step = rows // CHUNKS
    hidden = wg_hbm.shape[1]
    half = hidden // 2

    def device(x=x, zl=zl, zh=zh, y=y, core=core):
        return {"row": x * 2 + zl, "col": zh * 8 + y * 2 + core}

    to_core = device(core=other)
    to_next, to_prev = device(y=y_next), device(y=y_prev)
    to_zh, to_zl = device(zh=zo), device(zl=1 - zl)
    to_x = [device(x=(x + d) % 4) for d in (1, 2, 3)]
    from_x = [(x + 4 - d) % 4 for d in (1, 2, 3)]

    pending = []
    slots = {}

    def remote(name, j, src, dst, target):
        k = slots.setdefault(name, len(slots))
        return pltpu.make_async_remote_copy(
            src_ref=src, dst_ref=dst, send_sem=send_sem.at[k, j], recv_sem=recv_sem.at[k, j],
            device_id=target, device_id_type=MESH,
        )

    def send(name, j, src, dst, target):
        copy = remote(name, j, src, dst, target)
        copy.start()
        pending.append(copy)

    def arrive(name, j, dst):
        remote(name, j, dst, dst, to_core).wait_recv()

    weights = []
    for i, (src, dst) in enumerate(((wg_hbm, wg), (wu_hbm, wu), (wd_hbm, wd))):
        weights.append(pltpu.make_async_copy(src, dst, weight_sem.at[i]))
    loads = []
    for j in range(CHUNKS):
        for i, src in enumerate((x_hbm, og_hbm)):
            loads.append(
                pltpu.make_async_copy(
                    src.at[pl.ds(j * step, step)], xo.at[j, x, zl, i], load_sem.at[i, j]
                )
            )
    for copy in loads + weights:
        copy.start()

    barrier = pltpu.get_barrier_semaphore()
    peers = [to_core, to_next, to_prev, to_zh, to_zl] + to_x
    for peer in peers:
        pl.semaphore_signal(barrier, inc=1, device_id=peer, device_id_type=MESH)
    pl.semaphore_wait(barrier, len(peers))

    def gather_own(j):
        loads[2 * j].wait()
        loads[2 * j + 1].wait()
        mine = xo.at[j, x, zl]
        send("row_z", j, mine, mine, to_zl)
        for d in range(3):
            send(f"row_x{d}", j, mine, mine, to_x[d])

    def gather_pair(j):
        theirs = xo.at[j, x, 1 - zl]
        arrive("row_z", j, theirs)
        for d in range(3):
            send(f"row_xz{d}", j, theirs, theirs, to_x[d])

    stores = []

    def store(src, dst, a, j):
        copy = pltpu.make_async_copy(src, dst, store_sem.at[a, j])
        copy.start()
        stores.append(copy)

    def products(j):
        for d in range(3):
            arrive(f"row_x{d}", j, xo.at[j, from_x[d], zl])
            arrive(f"row_xz{d}", j, xo.at[j, from_x[d], 1 - zl])
        for a, (w, i, dims) in enumerate(((wg, 0, NN), (wu, 0, NN), (wd, 1, NT))):
            if j == 0:
                weights[a].wait()
            left = xo[j, :, :, i].reshape(8 * step, width)
            for t in range(2):
                cols = slice(t * half, (t + 1) * half)
                right = w[:, cols] if dims == NN else w[cols, :]
                value = dot(left, right, dims).astype(BF16)
                part[j, :, :, :, a, :, cols] = value.reshape(2, 4, 2, 16, half)
            send(f"core_in{a}", j, part.at[j, other, :, :, a], core_in.at[j, :, :, a], to_core)
        store(xo.at[j, :, :, 0], xf_out.at[j], 0, j)
        store(xo.at[j, :, :, 1], of_out.at[j], 1, j)

    def core_sum(j):
        for a in range(3):
            arrive(f"core_in{a}", j, core_in.at[j, :, :, a])
        pair = slice(0, 2)

        def add(yy, zz, arrays):
            part[j, core, yy, zz, arrays] += core_in[j, yy, zz, arrays]

        for z in range(2):
            add(y_far, z, pair)
        send("y1b+", j, part.at[j, core, y_far, 0, pair], y1b.at[j, 0], to_next)
        send("y1b-", j, part.at[j, core, y_far, 1, pair], y1b.at[j, 1], to_prev)
        for yy in range(4):
            add(yy, zo, 2)
        send("za", j, part.at[j, core, :, zo, 2], za.at[j], to_zh)
        add(y_next, 1, pair)
        send("y2b+e", j, part.at[j, core, y_next, 1, pair], y2b.at[j, 0, 1], to_next)
        add(y_prev, 0, pair)
        send("y2b-e", j, part.at[j, core, y_prev, 0, pair], y2b.at[j, 1, 0], to_prev)
        add(y_next, 0, pair)
        add(y_prev, 1, pair)
        add(y, 0, pair)
        add(y, 1, pair)
        for yy in range(4):
            add(yy, zh, 2)

    low, high = slice(0, half), slice(half, hidden)

    def first_sum(j):
        pair = slice(0, 2)
        arrive("y1b+", j, y1b.at[j, 0])
        part[j, core, y_next, 0, pair] += y1b[j, 0]
        send("y2b+l", j, part.at[j, core, y_next, 0, pair], y2b.at[j, 0, 0], to_next)
        arrive("y1b-", j, y1b.at[j, 1])
        part[j, core, y_prev, 1, pair] += y1b[j, 1]
        send("y2b-l", j, part.at[j, core, y_prev, 1, pair], y2b.at[j, 1, 1], to_prev)
        arrive("za", j, za.at[j])
        part[j, core, y_far, zh, 2] += za[j, y_far]
        send("y1a+", j, part.at[j, core, y_far, zh, 2, :, low], y1a.at[j, 0], to_next)
        send("y1a-", j, part.at[j, core, y_far, zh, 2, :, high], y1a.at[j, 1], to_prev)
        part[j, core, y_next, zh, 2] += za[j, y_next]
        send("y2a+e", j, part.at[j, core, y_next, zh, 2, :, high], y2a.at[j, 0, :, high], to_next)
        part[j, core, y_prev, zh, 2] += za[j, y_prev]
        send("y2a-e", j, part.at[j, core, y_prev, zh, 2, :, low], y2a.at[j, 1, :, low], to_prev)

    def second_sum(j):
        pair = slice(0, 2)
        arrive("y1a+", j, y1a.at[j, 0])
        part[j, core, y_next, zh, 2, :, low] += y1a[j, 0]
        send("y2a+l", j, part.at[j, core, y_next, zh, 2, :, low], y2a.at[j, 0, :, low], to_next)
        arrive("y1a-", j, y1a.at[j, 1])
        part[j, core, y_prev, zh, 2, :, high] += y1a[j, 1]
        send("y2a-l", j, part.at[j, core, y_prev, zh, 2, :, high], y2a.at[j, 1, :, high], to_prev)
        arrive("y2b+e", j, y2b.at[j, 0, 1])
        arrive("y2b+l", j, y2b.at[j, 0, 0])
        arrive("y2b-e", j, y2b.at[j, 1, 0])
        arrive("y2b-l", j, y2b.at[j, 1, 1])
        total = part[j, core, y, zo, pair].astype(F32) + y2b[j, 0, zo].astype(F32)
        part[j, core, y, zo, pair] = (total + y2b[j, 1, zo].astype(F32)).astype(BF16)
        send("zb", j, part.at[j, core, y, zo, pair], zb.at[j], to_zh)

    def activations(j):
        arrive("y2a+e", j, y2a.at[j, 0, :, high])
        arrive("y2a+l", j, y2a.at[j, 0, :, low])
        arrive("y2a-e", j, y2a.at[j, 1, :, low])
        arrive("y2a-l", j, y2a.at[j, 1, :, high])
        arrive("zb", j, zb.at[j])
        tile = hidden // 4
        for t in range(4):
            cols = slice(t * tile, (t + 1) * tile)

            def term(*refs):
                total = refs[0].astype(F32)
                for ref in refs[1:]:
                    total = total + ref.astype(F32)
                return total

            gate, up = (
                term(
                    part[j, core, y, zh, a, :, cols], y2b[j, 0, zh, a, :, cols],
                    y2b[j, 1, zh, a, :, cols], zb[j, a, :, cols],
                )
                for a in range(2)
            )
            act_grad = term(
                part[j, core, y, zh, 2, :, cols], za[j, y, :, cols],
                y2a[j, 0, :, cols], y2a[j, 1, :, cols],
            )
            act, slope = silu_parts(gate)
            full[j, core, y, zh, 0, :, cols] = (act * up).astype(BF16)
            full[j, core, y, zh, 1, :, cols] = (act_grad * up * slope).astype(BF16)
            full[j, core, y, zh, 2, :, cols] = (act_grad * act).astype(BF16)
        mine, last = full.at[j, core, y, zh, pl.ds(0, 2)], full.at[j, core, y, zh, 2]
        send("gzb", j, mine, mine, to_zh)
        send("gyb+o", j, mine, mine, to_next)
        send("gyb-o", j, mine, mine, to_prev)
        send("gya+", j, last, last, to_next)
        send("gya-", j, last, last, to_prev)
        send("gza_o", j, last, last, to_zh)
        own = full.at[j, core, y, zh]
        send("gc_o", j, own, own, to_core)

    def spread_z(j):
        theirs = full.at[j, core, y, zo, pl.ds(0, 2)]
        arrive("gzb", j, theirs)
        send("gyb+z", j, theirs, theirs, to_next)
        send("gyb-z", j, theirs, theirs, to_prev)
        send("gc_z", j, theirs, theirs, to_core)
        for name, yy, cols, target in (("+", y_prev, low, to_next), ("-", y_next, high, to_prev)):
            piece = full.at[j, core, yy, zh, 2]
            arrive("gya" + name, j, piece)
            send("gfa" + name, j, piece.at[:, cols], piece.at[:, cols], target)
            send("gza" + name, j, piece, piece, to_zh)
            send("gca" + name, j, piece, piece, to_core)

    def spread_y(j):
        pair = pl.ds(0, 2)
        for name, yy, z, target in (("+", y_prev, 0, to_next), ("-", y_next, 1, to_prev)):
            arrive(f"gyb{name}o", j, full.at[j, core, yy, zh, pair])
            arrive(f"gyb{name}z", j, full.at[j, core, yy, zo, pair])
            piece = full.at[j, core, yy, z, pair]
            send("gfb" + name, j, piece, piece, target)
            both = full.at[j, core, yy, :, pair]
            send("gcb" + name, j, both, both, to_core)
        far = full.at[j, core, y_far, zh, 2]
        arrive("gfa+", j, far.at[:, low])
        arrive("gfa-", j, far.at[:, high])
        send("gza_f", j, far, far, to_zh)
        send("gca_f", j, far, far, to_core)

    def spread_core(j):
        pair = pl.ds(0, 2)
        arrive("gfb+", j, full.at[j, core, y_far, 0, pair])
        arrive("gfb-", j, full.at[j, core, y_far, 1, pair])
        both = full.at[j, core, y_far, :, pair]
        send("gcb_f", j, both, both, to_core)
        arrive("gza_o", j, full.at[j, core, y, zo, 2])
        arrive("gza+", j, full.at[j, core, y_prev, zo, 2])
        arrive("gza-", j, full.at[j, core, y_next, zo, 2])
        arrive("gza_f", j, full.at[j, core, y_far, zo, 2])
        rest = full.at[j, core, :, zo, 2]
        send("gca_z", j, rest, rest, to_core)

    def outputs(j):
        pair = pl.ds(0, 2)
        arrive("gc_o", j, full.at[j, other, y, zh])
        arrive("gc_z", j, full.at[j, other, y, zo, pair])
        arrive("gca+", j, full.at[j, other, y_prev, zh, 2])
        arrive("gca-", j, full.at[j, other, y_next, zh, 2])
        arrive("gcb+", j, full.at[j, other, y_prev, :, pair])
        arrive("gcb-", j, full.at[j, other, y_next, :, pair])
        arrive("gca_f", j, full.at[j, other, y_far, zh, 2])
        arrive("gcb_f", j, full.at[j, other, y_far, :, pair])
        arrive("gca_z", j, full.at[j, other, :, zo, 2])
        for a, dst in enumerate((h_out, gg_out, ug_out)):
            store(full.at[j, :, :, :, a], dst.at[j], 2 + a, j)
        h, gg, ug = (full[j, :, :, :, a].reshape(8 * step, hidden) for a in range(3))
        shape = (4, 2, step, width)
        mix[j, :, :, 0] = dot(h, wd[...], NN).astype(BF16).reshape(shape)
        total = dot(gg, wg[...], NT) + dot(ug, wu[...], NT)
        mix[j, :, :, 1] = total.astype(BF16).reshape(shape)
        for d in range(3):
            send(f"mix_x{d}", j, mix.at[j, (x + d + 1) % 4], mix_x.at[j, d], to_x[d])

    def row_sum(j):
        for d in range(3):
            arrive(f"mix_x{d}", j, mix_x.at[j, d])

        def total(z):
            value = mix[j, x, z].astype(F32)
            for d in range(3):
                value = value + mix_x[j, d, z].astype(F32)
            return value

        mix[j, x, 1 - zl] = total(1 - zl).astype(BF16)
        send("mix_z", j, mix.at[j, x, 1 - zl], mix_z.at[j], to_zl)

    def finish(j):
        value = mix[j, x, zl].astype(F32)
        for d in range(3):
            value = value + mix_x[j, d, zl].astype(F32)
        arrive("mix_z", j, mix_z.at[j])
        outs[:, j] = (value + mix_z[j].astype(F32)).astype(BF16)

    stages = [products, core_sum, first_sum, second_sum, activations, spread_z, spread_y, spread_core, outputs, row_sum, finish]
    gather_own(0)
    gather_pair(0)
    gather_own(1)
    gather_pair(1)
    for t in range(2 * (CHUNKS - 1) + len(stages)):
        for j in range(CHUNKS):
            if 0 <= t - 2 * j < len(stages):
                stages[t - 2 * j](j)
        if t == 0 or t == 2:
            gather_own(2 + t // 2)
            gather_pair(2 + t // 2)

    final = [
        pltpu.make_async_copy(outs.at[i], dst, out_sem.at[i])
        for i, dst in enumerate((mix_out, gi_out))
    ]
    for copy in final:
        copy.start()
    for copy in pending:
        copy.wait_send()
    for copy in stores + final:
        copy.wait()


def exchange(inputs, gate_weight, up_weight, down_weight, out_grad):
    rows, width = inputs.shape
    hidden = gate_weight.shape[1]
    step = rows // CHUNKS

    def buffer(*shape):
        return pltpu.VMEM(shape, BF16)

    def out(*shape):
        return jax.ShapeDtypeStruct(shape, BF16)

    wide = out(CHUNKS, 2, 4, 2, 16, hidden)
    thin = out(CHUNKS, 4, 2, step, width)
    kinds = 56
    any_space = pl.BlockSpec(memory_space=pl.ANY)
    return pl.pallas_call(
        kernel,
        out_shape=(wide, wide, wide, thin, thin, out(CHUNKS, step, width), out(CHUNKS, step, width)),
        in_specs=[any_space] * 5,
        out_specs=[any_space] * 7,
        scratch_shapes=[
            buffer(CHUNKS, 4, 2, 2, step, width),
            buffer(width, hidden),
            buffer(width, hidden),
            buffer(hidden, width),
            buffer(CHUNKS, 2, 4, 2, 3, 16, hidden),
            buffer(CHUNKS, 4, 2, 3, 16, hidden),
            buffer(CHUNKS, 2, 2, 16, hidden),
            buffer(CHUNKS, 2, 2, 2, 16, hidden),
            buffer(CHUNKS, 2, 16, hidden),
            buffer(CHUNKS, 4, 16, hidden),
            buffer(CHUNKS, 2, 16, hidden // 2),
            buffer(CHUNKS, 2, 16, hidden),
            buffer(CHUNKS, 2, 4, 2, 3, 16, hidden),
            buffer(CHUNKS, 4, 2, 2, step, width),
            buffer(CHUNKS, 3, 2, 2, step, width),
            buffer(CHUNKS, 2, step, width),
            buffer(2, CHUNKS, step, width),
            pltpu.SemaphoreType.DMA((kinds, CHUNKS)),
            pltpu.SemaphoreType.DMA((kinds, CHUNKS)),
            pltpu.SemaphoreType.DMA((2, CHUNKS)),
            pltpu.SemaphoreType.DMA((3,)),
            pltpu.SemaphoreType.DMA((5, CHUNKS)),
            pltpu.SemaphoreType.DMA((2,)),
        ],
        compiler_params=pltpu.CompilerParams(
            collective_id=0, has_side_effects=True, vmem_limit_bytes=60 << 20
        ),
    )(inputs, out_grad, gate_weight, up_weight, down_weight)


def weight_kernel(tiles, x, og, gg, ug, h, grad_gate, grad_up, grad_down):
    i = pl.program_id(0)

    @pl.when(i < tiles)
    def _():
        grad_gate[...] = dot(x[...], gg[...], TN)

    @pl.when((i >= tiles) & (i < 2 * tiles))
    def _():
        grad_up[...] = dot(x[...], ug[...], TN)

    @pl.when(i >= 2 * tiles)
    def _():
        grad_down[...] = dot(h[...], og[...], TN)


def weight_grads(x, og, gg, ug, h):
    tokens, width = x.shape
    hidden = h.shape[1]
    tiles = 4
    tile = hidden // tiles

    def at(phase):
        return lambda i: jnp.clip(i - phase * tiles, 0, tiles - 1)

    def cols(phase):
        place = at(phase)
        return lambda i: (0, place(i))

    whole = pl.BlockSpec((tokens, width), lambda i: (0, 0))
    down = at(2)
    return pl.pallas_call(
        functools.partial(weight_kernel, tiles),
        grid=(3 * tiles,),
        out_shape=(
            jax.ShapeDtypeStruct((width, hidden), F32),
            jax.ShapeDtypeStruct((width, hidden), F32),
            jax.ShapeDtypeStruct((hidden, width), F32),
        ),
        in_specs=[whole, whole] + [pl.BlockSpec((tokens, tile), cols(p)) for p in range(3)],
        out_specs=[
            pl.BlockSpec((width, tile), cols(0)),
            pl.BlockSpec((width, tile), cols(1)),
            pl.BlockSpec((tile, width), lambda i: (down(i), 0)),
        ],
        compiler_params=pltpu.CompilerParams(vmem_limit_bytes=48 << 20),
    )(x, og, gg, ug, h)


def body(inputs, gate_weight, up_weight, down_weight, out_grad):
    h, gg, ug, x, og, mixed, grad_input = exchange(
        inputs, gate_weight, up_weight, down_weight, out_grad
    )
    rows, width = inputs.shape
    hidden = gate_weight.shape[1]
    grad_gate, grad_up, grad_down = weight_grads(
        x.reshape(-1, width), og.reshape(-1, width),
        gg.reshape(-1, hidden), ug.reshape(-1, hidden), h.reshape(-1, hidden),
    )
    return mixed.reshape(rows, width), grad_input.reshape(rows, width), grad_gate, grad_up, grad_down


def solution(mesh):
    in_specs = (P("row", "col"), P("col", "row"), P("col", "row"), P("row", "col"), P("row", "col"))
    out_specs = (
        P("row", "col"),
        P("row", "col"),
        P("col", "row"),
        P("col", "row"),
        P("row", "col"),
    )
    return jax.shard_map(body, mesh=mesh, in_specs=in_specs, out_specs=out_specs, check_vma=False)
```

time: 608 us -> 157 us (0.26)
  waiting for transfers between devices: 517 us -> 0 us
  Pallas kernels: 0 us -> 151 us
  matrix products: 56.4 us -> 0 us
  between operations: 14.2 us -> 0.65 us
  local copies, waits for them, and re-layouts: 12 us -> 3.76 us
    reduce_scatter x5 -> x0, waiting for transfers between devices: 289 us -> none  [the longest x1 84 us: body(): lax.psum_scatter(part_up.astype(jnp.bfloat16), 'col', scatter_dimension=0...]
    all_gather x5 -> x0, waiting for transfers between devices: 226 us -> none  [the longest x1 55.8 us: body(): lax.all_gather(gate_share, 'col', axis=0, tiled=True)]
    pallas_call x0 -> x2, Pallas kernels: none -> 151 us  [the longest x1 134 us: exchange(): pl.pallas_call(kernel, out_shape=(wide, wide, wide, thin, thin, out(CHUNK...]
    dot_general x9 -> x0, matrix products: 56.4 us -> none  [the longest x3 19.8 us: contract_first(): lax.dot_general(left, right, (((0,), (0,)), ((), ())), preferred_element_...]
    unnamed x8 -> x10, local copies, waits for them, and re-layouts: 12 us -> 3.76 us
  transfers between devices with their start and end apart: 10 -> 0, of which waited for: 9 -> 0; matrix products, arithmetic and copies ran while one was open for 11% -> 0% of each run, Pallas kernels for 0% -> 0%
where the time goes in v1:
time: 157 us; the launch traced here: 155 us
  Pallas kernels  151 us (96%)
  local copies, waits for them, and re-layouts  3.76 us (2%)
    pallas_call x1, Pallas kernels, exchange(): pl.pallas_call(kernel, out_shape=(wide, wide, wide, thin, thin, out(CHUNK...  134 us
    pallas_call x1, Pallas kernels, weight_grads(): pl.pallas_call(functools.partial(weight_kernel, tiles), grid=(3 * tiles,)...  16.6 us
    unnamed x10, local copies, waits for them, and re-layouts  3.76 us

profile of v1, /device:TPU:1, one launch (start us, length us, event | category | flops | bytes accessed | tf_op | source)
XLA Modules:
  0.0 155.0 jit_solution(945004657389424987)
XLA Ops:
  0.6 134.0 %shard_map.92 = (bf16[4,2,4,2,16,2048]{5,4,3,2,1,0:T(8,128)(2,1)}, bf16[4,2,4,2,16,2048]{5,4,3,2,1,0:T(8,128)(2,1)}, bf16[4,2,4,2,16,2048]{5,4,3,2,1,0:T(8,128)(...) custom-call(bf16[128,512]{1,0:T(8,128)(2,1)} %x_hbm.1, ...), custom_call_target="tpu_custom_call" | custom-call | tf_op jit(solution)/shard_map/pallas_call | solution.py:352
  134.6 0.0 copy-start
  134.7 1.2 copy-done
  135.9 0.0 copy-start.1
  135.9 1.2 copy-done.1
  137.1 0.0 copy-start.3
  137.1 0.0 copy-start.2
  137.1 16.6 %shard_map.93 = (f32[512,2048]{1,0:T(8,128)}, f32[512,2048]{1,0:T(8,128)}, f32[2048,512]{1,0:T(8,128)}) custom-call(bf16[1024,512]{1,0:T(8,128)(2,1)S(1)} %bitcast.7, bf16[1024,512]{1,0:T(8,128)(2,1)S(1)} %bitcast.8, bf16[1024,2048]{1,0:T(8,128)(2,1)} %bitcast.10, bf16[1024,2048]{1,0:T(8,128)(2,1)} %bitcast.11, bf16[1024,2048]{1,0:T(8,128)(2,1)} %bitcast.9), custom_call_target="tpu_custom_call" | custom-call | tf_op jit(solution)/shard_map/pallas_call | solution.py:419
  153.7 0.0 copy-done.3
  153.7 0.7 copy.12
  154.3 0.0 copy-done.2
  154.3 0.7 copy.13
Async XLA Ops:
  134.6 1.2 copy-start
  135.9 1.2 copy-start.1
  137.1 16.6 %copy-start.3 = (bf16[4,32,512]{2,1,0:T(8,128)(2,1)S(1)}, bf16[4,32,512]{2,1,0:T(8,128)(2,1)}, u32[]{:S(2)}) copy-start(bf16[4,32,512]{2,1,0:T(8,128)(2,1)} %get-tuple-element.15) | copy-start | bytes 393220
  137.1 17.2 %copy-start.2 = (bf16[4,32,512]{2,1,0:T(8,128)(2,1)S(1)}, bf16[4,32,512]{2,1,0:T(8,128)(2,1)}, u32[]{:S(2)}) copy-start(bf16[4,32,512]{2,1,0:T(8,128)(2,1)} %get-tuple-element.16) | copy-start | bytes 393220

commit v2 on v0

v2 whole, which is shorter than its diff:
```python
import functools

import jax
import jax.numpy as jnp
from jax import lax
from jax.experimental import pallas as pl
from jax.experimental.pallas import tpu as pltpu
from jax.sharding import PartitionSpec as P

MESH = pl.DeviceIdType.MESH
BF16, F32 = jnp.bfloat16, jnp.float32
PARTIAL = BF16
OFFSETS = ((0, 0), (0, 1), (2, 0), (1, 1), (3, 1), (2, 1), (1, 0), (3, 0))
CHUNKS = len(OFFSETS)
PAIR = OFFSETS.index((0, 1))
LATE = 2
COPIES = 260
NN = (((1,), (0,)), ((), ()))
NT = (((1,), (1,)), ((), ()))
TN = (((0,), (0,)), ((), ()))


def dot(left, right, dims):
    return lax.dot_general(left, right, dims, preferred_element_type=F32)


def silu_parts(gate):
    sig = jax.nn.sigmoid(gate)
    return gate * sig, sig * (1.0 + gate * (1.0 - sig))


ORDER = (
    ("R0", 0), ("G", 0), ("U", 0), ("R1", 0), ("A", 0), ("CB", 0), ("CA", 0), ("G", 6), ("U", 6), ("G", 1),
    ("FB+", 0), ("FB-", 0), ("U", 1), ("CB", 6), ("G", 2), ("A", 1), ("CB", 1), ("P0", 0), ("A", 6), ("FA", 0),
    ("SB", 0), ("FB+", 6), ("FB-", 6), ("A", 7), ("P1", 0), ("U", 2), ("CA", 6), ("G", 7), ("FB+", 1), ("FB-", 1),
    ("CB", 2), ("CA", 7), ("CA", 1), ("G", 3), ("SA+", 0), ("SA-", 0), ("U", 3), ("G", 4), ("SB", 6), ("U", 4),
    ("CB", 3), ("FA", 6), ("G", 5), ("FB-", 2), ("SB", 1), ("A", 3), ("A", 4), ("FA", 7), ("FB+", 2), ("U", 7),
    ("FB+", 3), ("FB-", 3), ("CA", 3), ("CA", 4), ("CB", 4), ("FA", 1), ("CB", 7), ("SA-", 6), ("SA+", 7),
    ("SA+", 6), ("A", 2), ("A", 5), ("SA-", 7), ("SB", 2), ("U", 5), ("SB", 3), ("CA", 5), ("CA", 2), ("FB+", 4),
    ("FB-", 4), ("FA", 3), ("CB", 5), ("SA+", 1), ("SA-", 1), ("FA", 4), ("FB-", 7), ("FB+", 7), ("SB", 4),
    ("SA-", 3), ("SA+", 3), ("FA", 5), ("FB+", 5), ("FB-", 5), ("FA", 2), ("SA+", 4), ("SA-", 4), ("SB", 7),
    ("ACT", 3), ("SA-", 5), ("SA+", 5), ("SB", 5), ("SA-", 2), ("SA+", 2), ("YA+", 3), ("YA-", 3), ("ACT", 7),
    ("ZB", 3), ("ACT", 2), ("ZF", 3), ("YA-", 7), ("YA+", 7), ("ZB", 7), ("YB-", 3), ("YB+", 3), ("ACT", 6),
    ("YA+", 2), ("YA-", 2), ("ZB", 2), ("ZF", 7), ("ZA", 3), ("YB+", 7), ("YB-", 7), ("ACT", 4), ("ZB", 6),
    ("MIX", 3), ("YA-", 6), ("YA+", 6), ("YF", 3), ("ZF", 2), ("ZA", 7), ("GI", 3), ("YB+", 2), ("YB-", 2),
    ("ACT", 5), ("ZB", 4), ("MIX", 7), ("YA-", 4), ("YA+", 4), ("YF", 7), ("ZA", 2), ("GI", 7), ("YB-", 6),
    ("ZB", 5), ("ZF", 6), ("YB+", 6), ("MIX", 2), ("YF", 2), ("YA-", 5), ("YA+", 5), ("GI", 2), ("YB+", 4),
    ("YB-", 4), ("ACT", 1), ("ZF", 4), ("ZA", 6), ("YB+", 5), ("MIX", 6), ("YF", 6), ("ZF", 5), ("YB-", 5),
    ("ACT", 0), ("YF", 4), ("ZB", 1), ("GI", 6), ("YA-", 1), ("YA+", 1), ("GI", 4), ("ZA", 4), ("YF", 5),
    ("YA+", 0), ("YA-", 0), ("MIX", 4), ("GI", 5), ("ZA", 5), ("YB-", 1), ("YB+", 1), ("ZB", 0), ("ZF", 1),
    ("ZF", 0), ("MIX", 5), ("W", 0), ("W", 0), ("W", 0), ("W", 0), ("YF", 1), ("W", 0), ("YB+", 0), ("YB-", 0),
    ("W", 0), ("GI", 1), ("ZA", 1), ("RS1", 0), ("W", 0), ("ZA", 0), ("MIX", 1), ("YF", 0), ("RS0", 0), ("MIX", 0),
    ("W", 0), ("GI", 0), ("W", 0), ("W", 0), ("FI1", 0), ("W", 0), ("W", 0), ("FI0", 0),
)


def kernel(
    x_hbm, og_hbm, wg_hbm, wu_hbm, wd_hbm,
    h_out, gg_out, ug_out, xf_out, of_out, mix_out, gi_out, gate_out, up_out, down_out,
    xo, wg, wu, wd, part, core_in, y1b, y2b, zb, za, y1a, y2a, full, mix, mix_in, mix_z, outs, wide_tiles, tall_tiles,
    send_sem, recv_sem, load_sem, weight_sem, store_sem, tile_sem, out_sem,
):
    row, col = lax.axis_index("row"), lax.axis_index("col")
    x, zl = row // 2, row % 2
    zh, y, core = col // 8, (col // 2) % 4, col % 2
    zo, other = 1 - zh, 1 - core
    y_next, y_prev, y_far = (y + 1) % 4, (y + 3) % 4, (y + 2) % 4
    rows, width = x_hbm.shape
    hidden = wg_hbm.shape[1]
    half = hidden // 2
    low, high = slice(0, half // 2), slice(half // 2, half)
    pair = pl.ds(0, 2)

    def device(x=x, zl=zl, zh=zh, y=y, core=core):
        return {"row": x * 2 + zl, "col": zh * 8 + y * 2 + core}

    to_core = device(core=other)
    to_next, to_prev = device(y=y_next), device(y=y_prev)
    to_zh, to_zl = device(zh=zo), device(zl=1 - zl)

    def along(d):
        return device(x=(x + d) % 4)

    pending = []
    slots = {}
    seen = set()

    def remote(name, j, src, dst, target):
        k = slots.setdefault((name, j), len(slots))
        return pltpu.make_async_remote_copy(
            src_ref=src, dst_ref=dst, send_sem=send_sem.at[k], recv_sem=recv_sem.at[k],
            device_id=target, device_id_type=MESH,
        )

    def send(name, j, src, dst, target):
        copy = remote(name, j, src, dst, target)
        copy.start()
        pending.append(copy)

    def arrive(name, j, dst):
        if (name, j) not in seen:
            seen.add((name, j))
            remote(name, j, dst, dst, to_core).wait_recv()

    stores = []

    def store(src, dst, sem):
        copy = pltpu.make_async_copy(src, dst, sem)
        copy.start()
        stores.append(copy)

    loads = [
        pltpu.make_async_copy(src, xo.at[0, i], load_sem.at[i])
        for i, src in enumerate((x_hbm, og_hbm))
    ]
    weights = [
        pltpu.make_async_copy(src, dst, weight_sem.at[i])
        for i, (src, dst) in enumerate(((wg_hbm, wg), (wu_hbm, wu), (wd_hbm, wd)))
    ]
    for copy in loads + weights:
        copy.start()

    barrier = pltpu.get_barrier_semaphore()
    peers = [to_core, to_next, to_prev, to_zh, to_zl] + [along(d) for d in (1, 2, 3)]
    for peer in peers:
        pl.semaphore_signal(barrier, inc=1, device_id=peer, device_id_type=MESH)
    pl.semaphore_wait(barrier, len(peers))

    def row_own(i):
        loads[i].wait()
        mine = xo.at[0, i]
        send(f"row{i}", PAIR, mine, xo.at[PAIR, i], to_zl)
        for d in (1, 3, 2):
            j = OFFSETS.index((d, 0))
            send(f"row{i}", j, mine, xo.at[j, i], along(4 - d))

    def row_pair(i):
        theirs = xo.at[PAIR, i]
        arrive(f"row{i}", PAIR, theirs)
        for d in (1, 3, 2):
            j = OFFSETS.index((d, 1))
            send(f"row{i}", j, theirs, xo.at[j, i], along(4 - d))

    def product(j, a, w, i, dims):
        if j == 0:
            weights[a].wait()
        else:
            arrive(f"row{i}", j, xo.at[j, i])
        left = xo[j, i]
        for c in range(2):
            cols = slice(c * half, (c + 1) * half)
            right = w[:, cols] if dims == NN else w[cols, :]
            part[j, c, :, :, a] = dot(left, right, dims).astype(BF16).reshape(4, 2, 16, half)
        send(f"core_in{a}", j, part.at[j, other, :, :, a], core_in.at[j, :, :, a], to_core)
        if a != 1 and j < LATE:
            store(xo.at[j, i], (xf_out, of_out)[i].at[j], store_sem.at[i, 0, j])

    def add(j, yy, zz, arrays):
        part[j, core, yy, zz, arrays] += core_in[j, yy, zz, arrays]

    def core_pair(j):
        for a in range(2):
            arrive(f"core_in{a}", j, core_in.at[j, :, :, a])
        both = slice(0, 2)
        add(j, y_far, 0, both)
        send("y1b+", j, part.at[j, core, y_far, 0, pair], y1b.at[j, 0], to_next)
        add(j, y_far, 1, both)
        send("y1b-", j, part.at[j, core, y_far, 1, pair], y1b.at[j, 1], to_prev)
        add(j, y_next, 1, both)
        send("y2b+e", j, part.at[j, core, y_next, 1, pair], y2b.at[j, 0, 1], to_next)
        add(j, y_prev, 0, both)
        send("y2b-e", j, part.at[j, core, y_prev, 0, pair], y2b.at[j, 1, 0], to_prev)
        add(j, y_next, 0, both)
        add(j, y_prev, 1, both)
        add(j, y, 0, both)
        add(j, y, 1, both)

    def first_next(j):
        arrive("y1b+", j, y1b.at[j, 0])
        part[j, core, y_next, 0, 0:2] += y1b[j, 0]
        send("y2b+l", j, part.at[j, core, y_next, 0, pair], y2b.at[j, 0, 0], to_next)

    def first_prev(j):
        arrive("y1b-", j, y1b.at[j, 1])
        part[j, core, y_prev, 1, 0:2] += y1b[j, 1]
        send("y2b-l", j, part.at[j, core, y_prev, 1, pair], y2b.at[j, 1, 1], to_prev)

    def second_pair(j):
        arrive("y2b+e", j, y2b.at[j, 0, 1])
        arrive("y2b+l", j, y2b.at[j, 0, 0])
        arrive("y2b-e", j, y2b.at[j, 1, 0])
        arrive("y2b-l", j, y2b.at[j, 1, 1])
        total = part[j, core, y, zo, 0:2].astype(F32) + y2b[j, 0, zo].astype(F32)
        part[j, core, y, zo, 0:2] = (total + y2b[j, 1, zo].astype(F32)).astype(BF16)
        send("zb", j, part.at[j, core, y, zo, pair], zb.at[j], to_zh)

    def core_last(j):
        arrive("core_in2", j, core_in.at[j, :, :, 2])
        for yy in range(4):
            add(j, yy, zo, 2)
        send("za", j, part.at[j, core, :, zo, 2], za.at[j], to_zh)
        for yy in range(4):
            add(j, yy, zh, 2)

    def first_last(j):
        arrive("za", j, za.at[j])
        part[j, core, y_far, zh, 2] += za[j, y_far]
        send("y1a+", j, part.at[j, core, y_far, zh, 2, :, low], y1a.at[j, 0], to_next)
        send("y1a-", j, part.at[j, core, y_far, zh, 2, :, high], y1a.at[j, 1], to_prev)
        part[j, core, y_next, zh, 2] += za[j, y_next]
        part[j, core, y_prev, zh, 2] += za[j, y_prev]

    def second_next(j):
        arrive("y1a+", j, y1a.at[j, 0])
        part[j, core, y_next, zh, 2, :, low] += y1a[j, 0]
        send("y2a+", j, part.at[j, core, y_next, zh, 2], y2a.at[j, 0], to_next)

    def second_prev(j):
        arrive("y1a-", j, y1a.at[j, 1])
        part[j, core, y_prev, zh, 2, :, high] += y1a[j, 1]
        send("y2a-", j, part.at[j, core, y_prev, zh, 2], y2a.at[j, 1], to_prev)

    def activations(j):
        arrive("y2a+", j, y2a.at[j, 0])
        arrive("y2a-", j, y2a.at[j, 1])
        arrive("zb", j, zb.at[j])
        for cols in (low, high):

            def term(*values):
                total = values[0].astype(F32)
                for value in values[1:]:
                    total = total + value.astype(F32)
                return total

            gate, up = (
                term(
                    part[j, core, y, zh, a, :, cols], y2b[j, 0, zh, a, :, cols],
                    y2b[j, 1, zh, a, :, cols], zb[j, a, :, cols],
                )
                for a in range(2)
            )
            act_grad = term(
                part[j, core, y, zh, 2, :, cols], za[j, y, :, cols],
                y2a[j, 0, :, cols], y2a[j, 1, :, cols],
            )
            act, slope = silu_parts(gate)
            full[j, core, y, zh, 0, :, cols] = (act_grad * up * slope).astype(BF16)
            full[j, core, y, zh, 1, :, cols] = (act_grad * act).astype(BF16)
            full[j, core, y, zh, 2, :, cols] = (act * up).astype(BF16)
        mine, single = full.at[j, core, y, zh, pair], full.at[j, core, y, zh, 2]
        send("gzb", j, mine, mine, to_zh)
        send("gya+", j, single, single, to_next)
        send("gya-", j, single, single, to_prev)
        send("gyb+o", j, mine, mine, to_next)
        send("gyb-o", j, mine, mine, to_prev)

    def spread_z(j):
        theirs = full.at[j, core, y, zo, pair]
        arrive("gzb", j, theirs)
        send("gyb+z", j, theirs, theirs, to_next)
        send("gyb-z", j, theirs, theirs, to_prev)

    def spread_single(j, name, yy, cols, target):
        piece = full.at[j, core, yy, zh, 2]
        arrive("gya" + name, j, piece)
        send("gfa" + name, j, piece.at[:, cols], piece.at[:, cols], target)

    def spread_pair(j, name, yy, z, target):
        arrive(f"gyb{name}o", j, full.at[j, core, yy, zh, pair])
        arrive(f"gyb{name}z", j, full.at[j, core, yy, zo, pair])
        piece = full.at[j, core, yy, z, pair]
        send("gfb" + name, j, piece, piece, target)

    def far_single(j):
        far = full.at[j, core, y_far, zh, 2]
        arrive("gfa+", j, far.at[:, low])
        arrive("gfa-", j, far.at[:, high])
        ring = full.at[j, core, :, zh, 2]
        send("gza", j, ring, ring, to_zh)

    def far_pair(j):
        arrive("gfb+", j, full.at[j, core, y_far, 0, pair])
        arrive("gfb-", j, full.at[j, core, y_far, 1, pair])
        whole = full.at[j, core, :, :, pair]
        send("gcb", j, whole, whole, to_core)

    def spread_rest(j):
        arrive("gza", j, full.at[j, core, :, zo, 2])
        whole = full.at[j, core, :, :, 2]
        send("gca", j, whole, whole, to_core)

    def send_mixed(j, i, value):
        mix[j, i] = value.astype(BF16)
        d = OFFSETS[j][0]
        if d:
            send(f"mix{i}", j, mix.at[j, i], mix_in.at[j, i], along(d))

    def acts(j, c, a):
        return full[j, c, :, :, a].reshape(rows, half)

    def store_acts(j, a, dst):
        if j < LATE:
            for c in range(2):
                store(
                    full.at[j, c, :, :, a], dst.at[j, :, :, :, pl.ds(c * half, half)],
                    store_sem.at[2 + a, c, j],
                )

    def output_mixed(j):
        arrive("gca", j, full.at[j, other, :, :, 2])
        value = dot(acts(j, 0, 2), wd[0:half, :], NN) + dot(acts(j, 1, 2), wd[half:hidden, :], NN)
        send_mixed(j, 0, value)
        store_acts(j, 2, h_out)

    def output_grad(j):
        arrive("gcb", j, full.at[j, other, :, :, pair])
        value = dot(acts(j, 0, 0), wg[:, 0:half], NT) + dot(acts(j, 1, 0), wg[:, half:hidden], NT)
        value = value + dot(acts(j, 0, 1), wu[:, 0:half], NT) + dot(acts(j, 1, 1), wu[:, half:hidden], NT)
        send_mixed(j, 1, value)
        store_acts(j, 0, gg_out)
        store_acts(j, 1, ug_out)

    def row_total(i, e):
        total = mix[OFFSETS.index((0, e)), i].astype(F32)
        for d in (1, 2, 3):
            j = OFFSETS.index((d, e))
            arrive(f"mix{i}", j, mix_in.at[j, i])
            total = total + mix_in[j, i].astype(F32)
        return total

    def row_sum(i):
        mix[PAIR, i] = row_total(i, 1).astype(BF16)
        send(f"mix_z{i}", 0, mix.at[PAIR, i], mix_z.at[i], to_zl)

    def finish(i):
        total = row_total(i, 0)
        arrive(f"mix_z{i}", 0, mix_z.at[i])
        outs[i] = (total + mix_z[i].astype(F32)).astype(BF16)
        store(outs.at[i], (mix_out, gi_out)[i], out_sem.at[i])

    done = []

    def weight_tile(k):
        tile = half // 2
        a, t = k // 4, k % 4
        units = full[LATE:, t // 2, :, :, a, :, (low, high)[t % 2]].reshape((CHUNKS - LATE) * rows, tile)
        side = xo[LATE:, a // 2].reshape((CHUNKS - LATE) * rows, width)
        if k >= 2:
            done[k - 2].wait()
        if a == 2:
            tall_tiles[k % 2] = dot(units, side, TN).astype(PARTIAL)
            src, dst = tall_tiles.at[k % 2], down_out.at[t]
        else:
            value = dot(side, units, TN).astype(PARTIAL)
            wide_tiles[k % 2] = value
            src, dst = wide_tiles.at[k % 2], (gate_out, up_out)[a].at[t]
        copy = pltpu.make_async_copy(src, dst, tile_sem.at[k])
        copy.start()
        done.append(copy)

    stages = {
        "R0": lambda j: row_own(0), "R1": lambda j: row_own(1),
        "P0": lambda j: row_pair(0), "P1": lambda j: row_pair(1),
        "G": lambda j: product(j, 0, wg, 0, NN),
        "U": lambda j: product(j, 1, wu, 0, NN),
        "A": lambda j: product(j, 2, wd, 1, NT),
        "CB": core_pair, "CA": core_last, "FB+": first_next, "FB-": first_prev, "FA": first_last,
        "SA+": second_next, "SA-": second_prev, "SB": second_pair, "ACT": activations, "ZB": spread_z,
        "YA+": lambda j: spread_single(j, "+", y_prev, low, to_next),
        "YA-": lambda j: spread_single(j, "-", y_next, high, to_prev),
        "YB+": lambda j: spread_pair(j, "+", y_prev, 0, to_next),
        "YB-": lambda j: spread_pair(j, "-", y_next, 1, to_prev),
        "ZF": far_single, "YF": far_pair, "ZA": spread_rest, "MIX": output_mixed, "GI": output_grad,
        "RS0": lambda j: row_sum(0), "RS1": lambda j: row_sum(1),
        "FI0": lambda j: finish(0), "FI1": lambda j: finish(1),
        "W": lambda j: weight_tile(len(done)),
    }
    for name, j in ORDER:
        stages[name](j)
    for copy in pending:
        copy.wait_send()
    for copy in stores + done[-2:]:
        copy.wait()


def exchange(inputs, gate_weight, up_weight, down_weight, out_grad):
    rows, width = inputs.shape
    hidden = gate_weight.shape[1]
    half = hidden // 2

    def buffer(*shape):
        return pltpu.VMEM(shape, BF16)

    def out(*shape, dtype=BF16):
        return jax.ShapeDtypeStruct(shape, dtype)

    wide = out(LATE, 4, 2, 16, hidden)
    thin = out(LATE, rows, width)
    own = out(rows, width)
    columns = out(4, width, hidden // 4, dtype=PARTIAL)
    any_space = pl.BlockSpec(memory_space=pl.ANY)
    outputs = (
        wide, wide, wide, thin, thin, own, own,
        columns, columns, out(4, hidden // 4, width, dtype=PARTIAL),
    )
    return pl.pallas_call(
        kernel,
        out_shape=outputs,
        in_specs=[any_space] * 5,
        out_specs=[any_space] * len(outputs),
        scratch_shapes=[
            buffer(CHUNKS, 2, rows, width),
            buffer(width, hidden),
            buffer(width, hidden),
            buffer(hidden, width),
            buffer(CHUNKS, 2, 4, 2, 3, 16, half),
            buffer(CHUNKS, 4, 2, 3, 16, half),
            buffer(CHUNKS, 2, 2, 16, half),
            buffer(CHUNKS, 2, 2, 2, 16, half),
            buffer(CHUNKS, 2, 16, half),
            buffer(CHUNKS, 4, 16, half),
            buffer(CHUNKS, 2, 16, half // 2),
            buffer(CHUNKS, 2, 16, half),
            buffer(CHUNKS, 2, 4, 2, 3, 16, half),
            buffer(CHUNKS, 2, rows, width),
            buffer(CHUNKS, 2, rows, width),
            buffer(2, rows, width),
            buffer(2, rows, width),
            pltpu.VMEM((2, width, hidden // 4), PARTIAL),
            pltpu.VMEM((2, hidden // 4, width), PARTIAL),
            pltpu.SemaphoreType.DMA((COPIES,)),
            pltpu.SemaphoreType.DMA((COPIES,)),
            pltpu.SemaphoreType.DMA((2,)),
            pltpu.SemaphoreType.DMA((3,)),
            pltpu.SemaphoreType.DMA((5, 2, LATE)),
            pltpu.SemaphoreType.DMA((12,)),
            pltpu.SemaphoreType.DMA((2,)),
        ],
        compiler_params=pltpu.CompilerParams(
            collective_id=0, has_side_effects=True, vmem_limit_bytes=62 << 20
        ),
    )(inputs, out_grad, gate_weight, up_weight, down_weight)


def weight_kernel(
    x_hbm, og_hbm, gg_hbm, ug_hbm, h_hbm, gate_hbm, up_hbm, down_hbm, mix_hbm, gi_hbm,
    mix_out, gi_out, gate_out, up_out, down_out,
    x, og, acts, parts, wide, tall, own, left_sem, part_sem, out_sem, own_sem,
):
    tiles, tile = wide.shape[1], wide.shape[3]
    pieces = ((x_hbm, x), (og_hbm, og), (gg_hbm, acts.at[0]), (ug_hbm, acts.at[1]), (h_hbm, acts.at[2]))
    loads = [pltpu.make_async_copy(src, dst, left_sem.at[i]) for i, (src, dst) in enumerate(pieces)]
    mine = [pltpu.make_async_copy(src, own.at[i], own_sem.at[i]) for i, src in enumerate((mix_hbm, gi_hbm))]
    sums = [
        [pltpu.make_async_copy(src.at[t], parts.at[a, t], part_sem.at[a, t]) for t in range(tiles)]
        for a, src in enumerate((gate_hbm, up_hbm, down_hbm))
    ]
    order = ((0, (0, 2)), (1, (3,)), (2, (1, 4)))
    for a, needs in order:
        for i in needs:
            loads[i].start()
        for copy in sums[a]:
            copy.start()
    for copy in mine:
        copy.start()
    stores = []
    for a, needs in order:
        for i in needs:
            loads[i].wait()
        for t in range(tiles):
            cols = slice(t * tile, (t + 1) * tile)
            sums[a][t].wait()
            if a == 2:
                tall[cols, :] = parts[a, t].astype(F32) + dot(acts[2, :, cols], og[...], TN)
                src, dst = tall.at[pl.ds(t * tile, tile)], down_out.at[pl.ds(t * tile, tile)]
            else:
                wide[a, t] = parts[a, t].astype(F32) + dot(x[...], acts[a, :, cols], TN)
                src, dst = wide.at[a, t], (gate_out, up_out)[a].at[:, pl.ds(t * tile, tile)]
            stores.append(pltpu.make_async_copy(src, dst, out_sem.at[a, t]))
            stores[-1].start()
    for i, copy in enumerate(mine):
        copy.wait()
        stores.append(pltpu.make_async_copy(own.at[i], (mix_out, gi_out)[i], own_sem.at[2 + i]))
        stores[-1].start()
    for copy in stores:
        copy.wait()


def weight_grads(x, og, gg, ug, h, gate_part, up_part, down_part, mixed, grad_input):
    tokens, width = x.shape
    hidden = h.shape[1]
    tiles = gate_part.shape[0]
    tile = hidden // tiles
    any_space = pl.BlockSpec(memory_space=pl.ANY)
    return pl.pallas_call(
        weight_kernel,
        out_shape=(
            jax.ShapeDtypeStruct(mixed.shape, BF16),
            jax.ShapeDtypeStruct(mixed.shape, BF16),
            jax.ShapeDtypeStruct((width, hidden), F32),
            jax.ShapeDtypeStruct((width, hidden), F32),
            jax.ShapeDtypeStruct((hidden, width), F32),
        ),
        in_specs=[any_space] * 10,
        out_specs=[any_space] * 5,
        scratch_shapes=[
            pltpu.VMEM((tokens, width), BF16),
            pltpu.VMEM((tokens, width), BF16),
            pltpu.VMEM((3, tokens, hidden), BF16),
            pltpu.VMEM((3, tiles, width, tile), PARTIAL),
            pltpu.VMEM((2, tiles, width, tile), F32),
            pltpu.VMEM((hidden, width), F32),
            pltpu.VMEM((2,) + mixed.shape, BF16),
            pltpu.SemaphoreType.DMA((5,)),
            pltpu.SemaphoreType.DMA((3, tiles)),
            pltpu.SemaphoreType.DMA((3, tiles)),
            pltpu.SemaphoreType.DMA((4,)),
        ],
        compiler_params=pltpu.CompilerParams(vmem_limit_bytes=62 << 20),
    )(x, og, gg, ug, h, gate_part, up_part, down_part, mixed, grad_input)


def body(inputs, gate_weight, up_weight, down_weight, out_grad):
    h, gg, ug, x, og, mixed, grad_input, gate_part, up_part, down_part = exchange(
        inputs, gate_weight, up_weight, down_weight, out_grad
    )
    width = inputs.shape[1]
    hidden = gate_weight.shape[1]
    return weight_grads(
        x.reshape(-1, width), og.reshape(-1, width),
        gg.reshape(-1, hidden), ug.reshape(-1, hidden), h.reshape(-1, hidden),
        gate_part, up_part, down_part, mixed, grad_input,
    )


def solution(mesh):
    in_specs = (P("row", "col"), P("col", "row"), P("col", "row"), P("row", "col"), P("row", "col"))
    out_specs = (
        P("row", "col"),
        P("row", "col"),
        P("col", "row"),
        P("col", "row"),
        P("row", "col"),
    )
    return jax.shard_map(body, mesh=mesh, in_specs=in_specs, out_specs=out_specs, check_vma=False)
```

time: 608 us -> 128 us (0.21)
  waiting for transfers between devices: 517 us -> 0 us
  Pallas kernels: 0 us -> 127 us
  matrix products: 56.4 us -> 0 us
  between operations: 14.2 us -> 0.82 us
  local copies, waits for them, and re-layouts: 12 us -> 0 us
    reduce_scatter x5 -> x0, waiting for transfers between devices: 289 us -> none  [the longest x1 84 us: body(): lax.psum_scatter(part_up.astype(jnp.bfloat16), 'col', scatter_dimension=0...]
    all_gather x5 -> x0, waiting for transfers between devices: 226 us -> none  [the longest x1 55.8 us: body(): lax.all_gather(gate_share, 'col', axis=0, tiled=True)]
    pallas_call x0 -> x2, Pallas kernels: none -> 127 us  [the longest x1 119 us: exchange(): pl.pallas_call(kernel, out_shape=outputs, in_specs=[any_space] * 5, out_s...]
    dot_general x9 -> x0, matrix products: 56.4 us -> none  [the longest x3 19.8 us: contract_first(): lax.dot_general(left, right, (((0,), (0,)), ((), ())), preferred_element_...]
    unnamed x8 -> x0, local copies, waits for them, and re-layouts: 12 us -> none
  transfers between devices with their start and end apart: 10 -> 0, of which waited for: 9 -> 0; matrix products, arithmetic and copies ran while one was open for 11% -> 0% of each run, Pallas kernels for 0% -> 0%
where the time goes in v2:
time: 128 us
  Pallas kernels  127 us (99%)
    pallas_call x1, Pallas kernels, exchange(): pl.pallas_call(kernel, out_shape=outputs, in_specs=[any_space] * 5, out_s...  119 us
    pallas_call x1, Pallas kernels, weight_grads(): pl.pallas_call(weight_kernel, out_shape=(jax.ShapeDtypeStruct(mixed.shape...  7.82 us

profile of v2, /device:TPU:1, one launch (start us, length us, event | category | flops | bytes accessed | tf_op | source)
XLA Modules:
  0.0 127.7 jit_solution(1047598897619797367)
XLA Ops:
  0.6 119.1 %shard_map.92 = (bf16[2,4,2,16,2048]{4,3,2,1,0:T(8,128)(2,1)}, bf16[2,4,2,16,2048]{4,3,2,1,0:T(8,128)(2,1)}, bf16[2,4,2,16,2048]{4,3,2,1,0:T(8,128)(2,1)}, bf16[...) custom-call(bf16[128,512]{1,0:T(8,128)(2,1)} %x_hbm.1, ...), custom_call_target="tpu_custom_call" | custom-call | tf_op jit(solution)/shard_map/pallas_call | solution.py:406
  119.7 7.8 %shard_map.93 = (bf16[128,512]{1,0:T(8,128)(2,1)}, bf16[128,512]{1,0:T(8,128)(2,1)}, f32[512,2048]{1,0:T(8,128)}, f32[512,2048]{1,0:T(8,128)}, f32[2048,512]{1,0:T(8,128)}) custom-call(bf16[256,512]{1,0:T(8,128)(2,1)} %bitcast.8, bf16[256,512]{1,0:T(8,128)(2,1)} %bitcast.9, bf16[256,2048]{1,0:T(8,128)(2,1)} %bitcast.6, bf16[256,2048]{1,0:T(8,128)(2,1)} %bitcast.7, ...), custom_call_target="tpu_custom_call" | custom-call | tf_op jit(solution)/shard_map/pallas_call | solution.py:495

commit v3 on v2

--- a/solution.py
+++ b/solution.py
@@ -10,13 +10,14 @@
 MESH = pl.DeviceIdType.MESH
 BF16, F32 = jnp.bfloat16, jnp.float32
 PARTIAL = BF16
-OFFSETS = ((0, 0), (0, 1), (2, 0), (1, 1), (3, 1), (2, 1), (1, 0), (3, 0))
+OFFSETS = ((0, 0), (0, 1), (2, 1), (1, 1), (3, 1), (2, 0), (1, 0), (3, 0))
 CHUNKS = len(OFFSETS)
 PAIR = OFFSETS.index((0, 1))
 LATE = 2
-COPIES = 260
+DIRECT = ()
+COPIES = 270
+VMEM_LIMIT = 62 << 20
 NN = (((1,), (0,)), ((), ()))
-NT = (((1,), (1,)), ((), ()))
 TN = (((0,), (0,)), ((), ()))
 
 
@@ -30,34 +31,34 @@
 
 
 ORDER = (
-    ("R0", 0), ("G", 0), ("U", 0), ("R1", 0), ("A", 0), ("CB", 0), ("CA", 0), ("G", 6), ("U", 6), ("G", 1),
-    ("FB+", 0), ("FB-", 0), ("U", 1), ("CB", 6), ("G", 2), ("A", 1), ("CB", 1), ("P0", 0), ("A", 6), ("FA", 0),
-    ("SB", 0), ("FB+", 6), ("FB-", 6), ("A", 7), ("P1", 0), ("U", 2), ("CA", 6), ("G", 7), ("FB+", 1), ("FB-", 1),
-    ("CB", 2), ("CA", 7), ("CA", 1), ("G", 3), ("SA+", 0), ("SA-", 0), ("U", 3), ("G", 4), ("SB", 6), ("U", 4),
-    ("CB", 3), ("FA", 6), ("G", 5), ("FB-", 2), ("SB", 1), ("A", 3), ("A", 4), ("FA", 7), ("FB+", 2), ("U", 7),
-    ("FB+", 3), ("FB-", 3), ("CA", 3), ("CA", 4), ("CB", 4), ("FA", 1), ("CB", 7), ("SA-", 6), ("SA+", 7),
-    ("SA+", 6), ("A", 2), ("A", 5), ("SA-", 7), ("SB", 2), ("U", 5), ("SB", 3), ("CA", 5), ("CA", 2), ("FB+", 4),
-    ("FB-", 4), ("FA", 3), ("CB", 5), ("SA+", 1), ("SA-", 1), ("FA", 4), ("FB-", 7), ("FB+", 7), ("SB", 4),
-    ("SA-", 3), ("SA+", 3), ("FA", 5), ("FB+", 5), ("FB-", 5), ("FA", 2), ("SA+", 4), ("SA-", 4), ("SB", 7),
-    ("ACT", 3), ("SA-", 5), ("SA+", 5), ("SB", 5), ("SA-", 2), ("SA+", 2), ("YA+", 3), ("YA-", 3), ("ACT", 7),
-    ("ZB", 3), ("ACT", 2), ("ZF", 3), ("YA-", 7), ("YA+", 7), ("ZB", 7), ("YB-", 3), ("YB+", 3), ("ACT", 6),
-    ("YA+", 2), ("YA-", 2), ("ZB", 2), ("ZF", 7), ("ZA", 3), ("YB+", 7), ("YB-", 7), ("ACT", 4), ("ZB", 6),
-    ("MIX", 3), ("YA-", 6), ("YA+", 6), ("YF", 3), ("ZF", 2), ("ZA", 7), ("GI", 3), ("YB+", 2), ("YB-", 2),
-    ("ACT", 5), ("ZB", 4), ("MIX", 7), ("YA-", 4), ("YA+", 4), ("YF", 7), ("ZA", 2), ("GI", 7), ("YB-", 6),
-    ("ZB", 5), ("ZF", 6), ("YB+", 6), ("MIX", 2), ("YF", 2), ("YA-", 5), ("YA+", 5), ("GI", 2), ("YB+", 4),
-    ("YB-", 4), ("ACT", 1), ("ZF", 4), ("ZA", 6), ("YB+", 5), ("MIX", 6), ("YF", 6), ("ZF", 5), ("YB-", 5),
-    ("ACT", 0), ("YF", 4), ("ZB", 1), ("GI", 6), ("YA-", 1), ("YA+", 1), ("GI", 4), ("ZA", 4), ("YF", 5),
-    ("YA+", 0), ("YA-", 0), ("MIX", 4), ("GI", 5), ("ZA", 5), ("YB-", 1), ("YB+", 1), ("ZB", 0), ("ZF", 1),
-    ("ZF", 0), ("MIX", 5), ("W", 0), ("W", 0), ("W", 0), ("W", 0), ("YF", 1), ("W", 0), ("YB+", 0), ("YB-", 0),
-    ("W", 0), ("GI", 1), ("ZA", 1), ("RS1", 0), ("W", 0), ("ZA", 0), ("MIX", 1), ("YF", 0), ("RS0", 0), ("MIX", 0),
-    ("W", 0), ("GI", 0), ("W", 0), ("W", 0), ("FI1", 0), ("W", 0), ("W", 0), ("FI0", 0),
+    ("R0", 0), ("G", 0), ("U", 0), ("R1", 0), ("A", 0), ("CB", 0), ("CA", 0), ("G", 6), ("P0", 0), ("G", 1),
+    ("U", 1), ("FB+", 0), ("FB-", 0), ("U", 6), ("G", 7), ("CB", 1), ("G", 5), ("T0", 0), ("CB", 6), ("A", 1),
+    ("SB", 0), ("FA", 0), ("P1", 0), ("U", 5), ("CA", 1), ("FB-", 1), ("U", 7), ("T1", 0), ("CB", 5), ("A", 5),
+    ("FB+", 6), ("FB-", 6), ("CB", 7), ("FB+", 1), ("G", 4), ("SA+", 0), ("CA", 5), ("U", 4), ("G", 3), ("FA", 1),
+    ("FB+", 5), ("U", 3), ("CB", 4), ("FB-", 5), ("A", 7), ("CB", 3), ("SA-", 0), ("A", 6), ("A", 4), ("CA", 7),
+    ("A", 3), ("FB+", 7), ("CA", 6), ("CA", 4), ("SB", 6), ("FA", 5), ("CA", 3), ("G", 2), ("U", 2), ("SA-", 1),
+    ("A", 2), ("SA+", 1), ("SB", 1), ("FB-", 4), ("CB", 2), ("FB-", 7), ("FA", 7), ("CA", 2), ("FB+", 4), ("SB", 5),
+    ("FA", 6), ("FB-", 3), ("FB+", 3), ("SA-", 5), ("FA", 4), ("SA+", 5), ("FB-", 2), ("FB+", 2), ("FA", 3),
+    ("SA+", 7), ("SB", 7), ("SA-", 7), ("SB", 4), ("SA-", 6), ("SA+", 6), ("SB", 3), ("SA+", 4), ("FA", 2),
+    ("SA-", 4), ("ACT", 5), ("SB", 2), ("SA+", 3), ("SA-", 3), ("SA-", 2), ("ACT", 4), ("YA+", 5), ("SA+", 2),
+    ("YA-", 5), ("ACT", 3), ("YA+", 4), ("YA-", 4), ("ZB", 4), ("ZF", 5), ("ACT", 2), ("YA-", 3), ("YA+", 3),
+    ("ZB", 3), ("ZF", 4), ("YB-", 4), ("YB+", 4), ("ACT", 1), ("YA-", 2), ("YA+", 2), ("ZA", 5), ("ZF", 3),
+    ("ZB", 2), ("MIX", 5), ("YB+", 3), ("YB-", 3), ("ACT", 7), ("YF", 4), ("YA-", 1), ("ZA", 4), ("YA+", 1),
+    ("GI", 4), ("ZF", 2), ("MIX", 4), ("YB-", 2), ("YB+", 2), ("ACT", 6), ("ZA", 3), ("YF", 3), ("YA-", 7),
+    ("YA+", 7), ("ZB", 7), ("MIX", 3), ("GI", 3), ("ZF", 1), ("ZA", 2), ("YF", 2), ("ZB", 5), ("YA-", 6),
+    ("YA+", 6), ("ZB", 6), ("MIX", 2), ("GI", 2), ("ZF", 7), ("YB-", 7), ("YB+", 7), ("ZA", 1), ("YB-", 5),
+    ("YB+", 5), ("ACT", 0), ("ZF", 6), ("MIX", 1), ("YB-", 6), ("YB+", 6), ("YF", 7), ("ZA", 7), ("RS0", 0),
+    ("YF", 5), ("ZB", 1), ("GI", 7), ("MIX", 7), ("YA-", 0), ("YA+", 0), ("GI", 5), ("ZA", 6), ("YF", 6), ("ZB", 0),
+    ("MIX", 6), ("YB-", 1), ("YB+", 1), ("GI", 6), ("ZF", 0), ("W", 0), ("YB+", 0), ("W", 0), ("YB-", 0), ("W", 0),
+    ("W", 0), ("YF", 1), ("W", 0), ("W", 0), ("W", 0), ("GI", 1), ("ZA", 0), ("RS1", 0), ("YF", 0), ("W", 0),
+    ("MIX", 0), ("FI0", 0), ("GI", 0), ("W", 0), ("W", 0), ("W", 0), ("FI1", 0), ("W", 0),
 )
 
 
 def kernel(
     x_hbm, og_hbm, wg_hbm, wu_hbm, wd_hbm,
     h_out, gg_out, ug_out, xf_out, of_out, mix_out, gi_out, gate_out, up_out, down_out,
-    xo, wg, wu, wd, part, core_in, y1b, y2b, zb, za, y1a, y2a, full, mix, mix_in, mix_z, outs, wide_tiles, tall_tiles,
+    xo, wg, wu, wd, wgt, wut, wdt, part, core_in, y1b, y2b, zb, za, y1a, y2a, full, mix, mix_in, mix_z, outs, tiles,
     send_sem, recv_sem, load_sem, weight_sem, store_sem, tile_sem, out_sem,
 ):
     row, col = lax.axis_index("row"), lax.axis_index("col")
@@ -102,6 +103,14 @@
             seen.add((name, j))
             remote(name, j, dst, dst, to_core).wait_recv()
 
+    settled = []
+
+    def settle(count):
+        while len(settled) < count:
+            copy = pending[len(settled)]
+            copy.wait_send()
+            settled.append(copy)
+
     stores = []
 
     def store(src, dst, sem):
@@ -121,7 +130,8 @@
         copy.start()
 
     barrier = pltpu.get_barrier_semaphore()
-    peers = [to_core, to_next, to_prev, to_zh, to_zl] + [along(d) for d in (1, 2, 3)]
+    to_next_zh, to_prev_zh = device(zh=zo, y=y_next), device(zh=zo, y=y_prev)
+    peers = [to_core, to_next, to_prev, to_zh, to_zl, to_next_zh, to_prev_zh] + [along(d) for d in (1, 2, 3)]
     for peer in peers:
         pl.semaphore_signal(barrier, inc=1, device_id=peer, device_id_type=MESH)
     pl.semaphore_wait(barrier, len(peers))
@@ -141,17 +151,31 @@
             j = OFFSETS.index((d, 1))
             send(f"row{i}", j, theirs, xo.at[j, i], along(4 - d))
 
-    def product(j, a, w, i, dims):
+    def transpose(src, dst):
+        across = src.shape[0] < src.shape[1]
+        size = max(src.shape) // 8
+        for k in range(8):
+            block = slice(k * size, (k + 1) * size)
+            if across:
+                dst[block, :] = src[:, block].T
+            else:
+                dst[:, block] = src[block, :].T
+
+    def send_product(j, a):
+        send(f"core_in{a}", j, part.at[j, other, :, :, a], core_in.at[j, :, :, a], to_core)
+
+    def product(j, a, w, i):
         if j == 0:
             weights[a].wait()
+            if a == 2:
+                transpose(wd, wdt)
         else:
             arrive(f"row{i}", j, xo.at[j, i])
         left = xo[j, i]
         for c in range(2):
             cols = slice(c * half, (c + 1) * half)
-            right = w[:, cols] if dims == NN else w[cols, :]
-            part[j, c, :, :, a] = dot(left, right, dims).astype(BF16).reshape(4, 2, 16, half)
-        send(f"core_in{a}", j, part.at[j, other, :, :, a], core_in.at[j, :, :, a], to_core)
+            part[j, c, :, :, a] = dot(left, w[:, cols], NN).astype(BF16).reshape(4, 2, 16, half)
+        send_product(j, a)
         if a != 1 and j < LATE:
             store(xo.at[j, i], (xf_out, of_out)[i].at[j], store_sem.at[i, 0, j])
 
@@ -253,17 +277,24 @@
         send("gya-", j, single, single, to_prev)
         send("gyb+o", j, mine, mine, to_next)
         send("gyb-o", j, mine, mine, to_prev)
+        if j in DIRECT:
+            send("gyb+z", j, mine, mine, to_next_zh)
+            send("gyb-z", j, mine, mine, to_prev_zh)
+            send("gza_o", j, single, single, to_zh)
 
     def spread_z(j):
         theirs = full.at[j, core, y, zo, pair]
         arrive("gzb", j, theirs)
-        send("gyb+z", j, theirs, theirs, to_next)
-        send("gyb-z", j, theirs, theirs, to_prev)
+        if j not in DIRECT:
+            send("gyb+z", j, theirs, theirs, to_next)
+            send("gyb-z", j, theirs, theirs, to_prev)
 
     def spread_single(j, name, yy, cols, target):
         piece = full.at[j, core, yy, zh, 2]
         arrive("gya" + name, j, piece)
         send("gfa" + name, j, piece.at[:, cols], piece.at[:, cols], target)
+        if j in DIRECT:
+            send("gza" + name, j, piece, piece, to_zh)
 
     def spread_pair(j, name, yy, z, target):
         arrive(f"gyb{name}o", j, full.at[j, core, yy, zh, pair])
@@ -275,8 +306,11 @@
         far = full.at[j, core, y_far, zh, 2]
         arrive("gfa+", j, far.at[:, low])
         arrive("gfa-", j, far.at[:, high])
-        ring = full.at[j, core, :, zh, 2]
-        send("gza", j, ring, ring, to_zh)
+        if j in DIRECT:
+            send("gza_f", j, far, far, to_zh)
+        else:
+            ring = full.at[j, core, :, zh, 2]
+            send("gza", j, ring, ring, to_zh)
 
     def far_pair(j):
         arrive("gfb+", j, full.at[j, core, y_far, 0, pair])
@@ -285,7 +319,11 @@
         send("gcb", j, whole, whole, to_core)
 
     def spread_rest(j):
-        arrive("gza", j, full.at[j, core, :, zo, 2])
+        if j in DIRECT:
+            for name, yy in (("gza_o", y), ("gza+", y_prev), ("gza-", y_next), ("gza_f", y_far)):
+                arrive(name, j, full.at[j, core, yy, zo, 2])
+        else:
+            arrive("gza", j, full.at[j, core, :, zo, 2])
         whole = full.at[j, core, :, :, 2]
         send("gca", j, whole, whole, to_core)
 
@@ -293,7 +331,7 @@
         mix[j, i] = value.astype(BF16)
         d = OFFSETS[j][0]
         if d:
-            send(f"mix{i}", j, mix.at[j, i], mix_in.at[j, i], along(d))
+            send(f"mix{i}", j, mix.at[j, i], mix_in.at[j - 2, i], along(d))
 
     def acts(j, c, a):
         return full[j, c, :, :, a].reshape(rows, half)
@@ -314,8 +352,8 @@
 
     def output_grad(j):
         arrive("gcb", j, full.at[j, other, :, :, pair])
-        value = dot(acts(j, 0, 0), wg[:, 0:half], NT) + dot(acts(j, 1, 0), wg[:, half:hidden], NT)
-        value = value + dot(acts(j, 0, 1), wu[:, 0:half], NT) + dot(acts(j, 1, 1), wu[:, half:hidden], NT)
+        value = dot(acts(j, 0, 0), wgt[0:half, :], NN) + dot(acts(j, 1, 0), wgt[half:hidden, :], NN)
+        value = value + dot(acts(j, 0, 1), wut[0:half, :], NN) + dot(acts(j, 1, 1), wut[half:hidden, :], NN)
         send_mixed(j, 1, value)
         store_acts(j, 0, gg_out)
         store_acts(j, 1, ug_out)
@@ -324,8 +362,8 @@
         total = mix[OFFSETS.index((0, e)), i].astype(F32)
         for d in (1, 2, 3):
             j = OFFSETS.index((d, e))
-            arrive(f"mix{i}", j, mix_in.at[j, i])
-            total = total + mix_in[j, i].astype(F32)
+            arrive(f"mix{i}", j, mix_in.at[j - 2, i])
+            total = total + mix_in[j - 2, i].astype(F32)
         return total
 
     def row_sum(i):
@@ -348,22 +386,22 @@
         if k >= 2:
             done[k - 2].wait()
         if a == 2:
-            tall_tiles[k % 2] = dot(units, side, TN).astype(PARTIAL)
-            src, dst = tall_tiles.at[k % 2], down_out.at[t]
+            tiles[k % 2] = dot(units, side, TN).astype(PARTIAL)
+            dst = down_out.at[t]
         else:
-            value = dot(side, units, TN).astype(PARTIAL)
-            wide_tiles[k % 2] = value
-            src, dst = wide_tiles.at[k % 2], (gate_out, up_out)[a].at[t]
-        copy = pltpu.make_async_copy(src, dst, tile_sem.at[k])
+            tiles[k % 2] = dot(side, units, TN).astype(PARTIAL)
+            dst = (gate_out, up_out)[a].at[t]
+        copy = pltpu.make_async_copy(tiles.at[k % 2], dst, tile_sem.at[k])
         copy.start()
         done.append(copy)
 
     stages = {
         "R0": lambda j: row_own(0), "R1": lambda j: row_own(1),
         "P0": lambda j: row_pair(0), "P1": lambda j: row_pair(1),
-        "G": lambda j: product(j, 0, wg, 0, NN),
-        "U": lambda j: product(j, 1, wu, 0, NN),
-        "A": lambda j: product(j, 2, wd, 1, NT),
+        "G": lambda j: product(j, 0, wg, 0),
+        "U": lambda j: product(j, 1, wu, 0),
+        "A": lambda j: product(j, 2, wdt, 1),
+        "T0": lambda j: transpose(wg, wgt), "T1": lambda j: transpose(wu, wut),
         "CB": core_pair, "CA": core_last, "FB+": first_next, "FB-": first_prev, "FA": first_last,
         "SA+": second_next, "SA-": second_prev, "SB": second_pair, "ACT": activations, "ZB": spread_z,
         "YA+": lambda j: spread_single(j, "+", y_prev, low, to_next),
@@ -375,10 +413,13 @@
         "FI0": lambda j: finish(0), "FI1": lambda j: finish(1),
         "W": lambda j: weight_tile(len(done)),
     }
+    sent = []
     for name, j in ORDER:
         stages[name](j)
-    for copy in pending:
-        copy.wait_send()
+        sent.append(len(pending))
+        if len(sent) > 40:
+            settle(sent[-41])
+    settle(len(pending))
     for copy in stores + done[-2:]:
         copy.wait()
 
@@ -413,6 +454,9 @@
             buffer(width, hidden),
             buffer(width, hidden),
             buffer(hidden, width),
+            buffer(hidden, width),
+            buffer(hidden, width),
+            buffer(width, hidden),
             buffer(CHUNKS, 2, 4, 2, 3, 16, half),
             buffer(CHUNKS, 4, 2, 3, 16, half),
             buffer(CHUNKS, 2, 2, 16, half),
@@ -423,11 +467,10 @@
             buffer(CHUNKS, 2, 16, half),
             buffer(CHUNKS, 2, 4, 2, 3, 16, half),
             buffer(CHUNKS, 2, rows, width),
-            buffer(CHUNKS, 2, rows, width),
+            buffer(CHUNKS - 2, 2, rows, width),
             buffer(2, rows, width),
             buffer(2, rows, width),
             pltpu.VMEM((2, width, hidden // 4), PARTIAL),
-            pltpu.VMEM((2, hidden // 4, width), PARTIAL),
             pltpu.SemaphoreType.DMA((COPIES,)),
             pltpu.SemaphoreType.DMA((COPIES,)),
             pltpu.SemaphoreType.DMA((2,)),
@@ -437,7 +480,7 @@
             pltpu.SemaphoreType.DMA((2,)),
         ],
         compiler_params=pltpu.CompilerParams(
-            collective_id=0, has_side_effects=True, vmem_limit_bytes=62 << 20
+            collective_id=0, has_side_effects=True, vmem_limit_bytes=VMEM_LIMIT
         ),
     )(inputs, out_grad, gate_weight, up_weight, down_weight)
 
@@ -516,7 +559,7 @@
             pltpu.SemaphoreType.DMA((3, tiles)),
             pltpu.SemaphoreType.DMA((4,)),
         ],
-        compiler_params=pltpu.CompilerParams(vmem_limit_bytes=62 << 20),
+        compiler_params=pltpu.CompilerParams(vmem_limit_bytes=VMEM_LIMIT),
     )(x, og, gg, ug, h, gate_part, up_part, down_part, mixed, grad_input)
 
 

time: 128 us -> 124 us (0.969)
  Pallas kernels: 127 us -> 123 us
    pallas_call x1, Pallas kernels: 119 us -> 115 us  [exchange(): pl.pallas_call(kernel, out_shape=outputs, in_specs=[any_space] * 5, out_s...]
where the time goes in v3:
time: 124 us
  Pallas kernels  123 us (99%)
    pallas_call x1, Pallas kernels, exchange(): pl.pallas_call(kernel, out_shape=outputs, in_specs=[any_space] * 5, out_s...  115 us
    pallas_call x1, Pallas kernels, weight_grads(): pl.pallas_call(weight_kernel, out_shape=(jax.ShapeDtypeStruct(mixed.shape...  7.82 us

profile of v3, /device:TPU:1, one launch (start us, length us, event | category | flops | bytes accessed | tf_op | source)
XLA Modules:
  0.0 123.9 jit_solution(14200303615622442404)
XLA Ops:
  0.6 115.3 %shard_map.92 = (bf16[2,4,2,16,2048]{4,3,2,1,0:T(8,128)(2,1)}, bf16[2,4,2,16,2048]{4,3,2,1,0:T(8,128)(2,1)}, bf16[2,4,2,16,2048]{4,3,2,1,0:T(8,128)(2,1)}, bf16[...) custom-call(bf16[128,512]{1,0:T(8,128)(2,1)} %x_hbm.1, ...), custom_call_target="tpu_custom_call" | custom-call | tf_op jit(solution)/shard_map/pallas_call | solution.py:447
  115.9 7.8 %shard_map.93 = (bf16[128,512]{1,0:T(8,128)(2,1)}, bf16[128,512]{1,0:T(8,128)(2,1)}, f32[512,2048]{1,0:T(8,128)}, f32[512,2048]{1,0:T(8,128)}, f32[2048,512]{1,0:T(8,128)}) custom-call(bf16[256,512]{1,0:T(8,128)(2,1)} %bitcast.8, bf16[256,512]{1,0:T(8,128)(2,1)} %bitcast.9, bf16[256,2048]{1,0:T(8,128)(2,1)} %bitcast.6, bf16[256,2048]{1,0:T(8,128)(2,1)} %bitcast.7, ...), custom_call_target="tpu_custom_call" | custom-call | tf_op jit(solution)/shard_map/pallas_call | solution.py:538

commit v4 on v3

--- a/solution.py
+++ b/solution.py
@@ -14,6 +14,7 @@
 CHUNKS = len(OFFSETS)
 PAIR = OFFSETS.index((0, 1))
 LATE = 2
+SPLIT = 5
 DIRECT = ()
 COPIES = 270
 VMEM_LIMIT = 62 << 20
@@ -31,34 +32,35 @@
 
 
 ORDER = (
-    ("R0", 0), ("G", 0), ("U", 0), ("R1", 0), ("A", 0), ("CB", 0), ("CA", 0), ("G", 6), ("P0", 0), ("G", 1),
-    ("U", 1), ("FB+", 0), ("FB-", 0), ("U", 6), ("G", 7), ("CB", 1), ("G", 5), ("T0", 0), ("CB", 6), ("A", 1),
-    ("SB", 0), ("FA", 0), ("P1", 0), ("U", 5), ("CA", 1), ("FB-", 1), ("U", 7), ("T1", 0), ("CB", 5), ("A", 5),
-    ("FB+", 6), ("FB-", 6), ("CB", 7), ("FB+", 1), ("G", 4), ("SA+", 0), ("CA", 5), ("U", 4), ("G", 3), ("FA", 1),
-    ("FB+", 5), ("U", 3), ("CB", 4), ("FB-", 5), ("A", 7), ("CB", 3), ("SA-", 0), ("A", 6), ("A", 4), ("CA", 7),
-    ("A", 3), ("FB+", 7), ("CA", 6), ("CA", 4), ("SB", 6), ("FA", 5), ("CA", 3), ("G", 2), ("U", 2), ("SA-", 1),
-    ("A", 2), ("SA+", 1), ("SB", 1), ("FB-", 4), ("CB", 2), ("FB-", 7), ("FA", 7), ("CA", 2), ("FB+", 4), ("SB", 5),
-    ("FA", 6), ("FB-", 3), ("FB+", 3), ("SA-", 5), ("FA", 4), ("SA+", 5), ("FB-", 2), ("FB+", 2), ("FA", 3),
-    ("SA+", 7), ("SB", 7), ("SA-", 7), ("SB", 4), ("SA-", 6), ("SA+", 6), ("SB", 3), ("SA+", 4), ("FA", 2),
-    ("SA-", 4), ("ACT", 5), ("SB", 2), ("SA+", 3), ("SA-", 3), ("SA-", 2), ("ACT", 4), ("YA+", 5), ("SA+", 2),
-    ("YA-", 5), ("ACT", 3), ("YA+", 4), ("YA-", 4), ("ZB", 4), ("ZF", 5), ("ACT", 2), ("YA-", 3), ("YA+", 3),
-    ("ZB", 3), ("ZF", 4), ("YB-", 4), ("YB+", 4), ("ACT", 1), ("YA-", 2), ("YA+", 2), ("ZA", 5), ("ZF", 3),
-    ("ZB", 2), ("MIX", 5), ("YB+", 3), ("YB-", 3), ("ACT", 7), ("YF", 4), ("YA-", 1), ("ZA", 4), ("YA+", 1),
-    ("GI", 4), ("ZF", 2), ("MIX", 4), ("YB-", 2), ("YB+", 2), ("ACT", 6), ("ZA", 3), ("YF", 3), ("YA-", 7),
-    ("YA+", 7), ("ZB", 7), ("MIX", 3), ("GI", 3), ("ZF", 1), ("ZA", 2), ("YF", 2), ("ZB", 5), ("YA-", 6),
-    ("YA+", 6), ("ZB", 6), ("MIX", 2), ("GI", 2), ("ZF", 7), ("YB-", 7), ("YB+", 7), ("ZA", 1), ("YB-", 5),
-    ("YB+", 5), ("ACT", 0), ("ZF", 6), ("MIX", 1), ("YB-", 6), ("YB+", 6), ("YF", 7), ("ZA", 7), ("RS0", 0),
-    ("YF", 5), ("ZB", 1), ("GI", 7), ("MIX", 7), ("YA-", 0), ("YA+", 0), ("GI", 5), ("ZA", 6), ("YF", 6), ("ZB", 0),
-    ("MIX", 6), ("YB-", 1), ("YB+", 1), ("GI", 6), ("ZF", 0), ("W", 0), ("YB+", 0), ("W", 0), ("YB-", 0), ("W", 0),
-    ("W", 0), ("YF", 1), ("W", 0), ("W", 0), ("W", 0), ("GI", 1), ("ZA", 0), ("RS1", 0), ("YF", 0), ("W", 0),
-    ("MIX", 0), ("FI0", 0), ("GI", 0), ("W", 0), ("W", 0), ("W", 0), ("FI1", 0), ("W", 0),
+    ("R0", 0), ("R1", 0), ("G", 0), ("U", 0), ("A", 0), ("CB", 0), ("CA", 0), ("G", 1), ("U", 1), ("G", 7),
+    ("P0", 0), ("FB+", 0), ("FB-", 0), ("U", 7), ("CB", 1), ("T1", 0), ("G", 5), ("CB", 7), ("A", 1), ("G", 6),
+    ("U", 5), ("FA", 0), ("CA", 1), ("FB-", 1), ("A", 6), ("CB", 5), ("T0", 0), ("A", 5), ("CA", 6), ("FB+", 7),
+    ("FB-", 7), ("U", 6), ("P1", 0), ("CA", 5), ("G", 4), ("U", 4), ("CB", 6), ("FA", 1), ("FB+", 5), ("SA-", 0),
+    ("G", 3), ("CB", 4), ("FB-", 5), ("U", 3), ("G", 2), ("FA", 6), ("U", 2), ("SA+", 0), ("A", 4), ("FB+", 6),
+    ("A", 3), ("CB", 2), ("FA", 5), ("SA+", 1), ("FB-", 6), ("CA", 4), ("CA", 3), ("SB", 7), ("A", 2), ("SA-", 1),
+    ("FB+", 1), ("A", 7), ("FB+", 4), ("CB", 3), ("CA", 2), ("FB-", 4), ("SB", 0), ("CA", 7), ("SA+", 6), ("FA", 4),
+    ("SB", 5), ("SA-", 6), ("FB+", 2), ("FB-", 2), ("FA", 3), ("SA+", 5), ("SA-", 5), ("SB", 6), ("SB", 1),
+    ("FA", 2), ("FB-", 3), ("FB+", 3), ("SB", 4), ("SA-", 4), ("SA+", 4), ("FA", 7), ("SB", 2), ("SA+", 3),
+    ("SA-", 3), ("ACT", 5), ("SA+", 2), ("SA-", 2), ("SB", 3), ("SA+", 7), ("SA-", 7), ("ACT", 4), ("YA+", 5),
+    ("YA-", 5), ("ACT", 2), ("YA+", 4), ("ACT", 3), ("YA-", 4), ("ZB", 4), ("ZF", 5), ("YA+", 2), ("YA-", 2),
+    ("ZB", 2), ("YA-", 3), ("YA+", 3), ("ZB", 3), ("ZF", 4), ("YB+", 4), ("ZA", 5), ("YB-", 4), ("ACT", 1),
+    ("ZF", 2), ("MIX", 5), ("YB-", 2), ("YB+", 2), ("ZF", 3), ("ACT", 6), ("YB+", 3), ("YB-", 3), ("ACT", 7),
+    ("ZA", 4), ("YF", 4), ("YA+", 1), ("YA-", 1), ("MIX", 4), ("GI", 4), ("YF", 2), ("ZA", 2), ("ZB", 5),
+    ("YA+", 6), ("YA-", 6), ("GI", 2), ("ZA", 3), ("MIX", 2), ("YF", 3), ("YA+", 7), ("YA-", 7), ("ZB", 6),
+    ("MIX", 3), ("GI", 3), ("ZB", 7), ("ZF", 1), ("WA", 0), ("YB+", 5), ("YB-", 5), ("WA", 0), ("ZF", 6), ("ZF", 7),
+    ("WA", 0), ("WA", 0), ("WA", 0), ("YB+", 6), ("YB-", 6), ("WA", 0), ("WA", 0), ("WA", 0), ("WA", 0), ("YB-", 7),
+    ("YB+", 7), ("WA", 0), ("WA", 0), ("WA", 0), ("ZA", 1), ("YF", 5), ("ZB", 1), ("ACT", 0), ("YF", 6), ("MIX", 1),
+    ("RS0", 0), ("GI", 5), ("ZA", 6), ("YF", 7), ("GI", 6), ("YA-", 0), ("YB-", 1), ("YA+", 0), ("YB+", 1),
+    ("MIX", 6), ("ZA", 7), ("GI", 7), ("ZB", 0), ("MIX", 7), ("ZF", 0), ("WB", 0), ("WB", 0), ("YF", 1), ("WB", 0),
+    ("WB", 0), ("WB", 0), ("WB", 0), ("YB+", 0), ("YB-", 0), ("GI", 1), ("RS1", 0), ("WB", 0), ("WB", 0), ("ZA", 0),
+    ("WB", 0), ("WB", 0), ("WB", 0), ("YF", 0), ("MIX", 0), ("FI0", 0), ("WB", 0), ("GI", 0), ("FI1", 0),
 )
 
 
 def kernel(
     x_hbm, og_hbm, wg_hbm, wu_hbm, wd_hbm,
     h_out, gg_out, ug_out, xf_out, of_out, mix_out, gi_out, gate_out, up_out, down_out,
-    xo, wg, wu, wd, wgt, wut, wdt, part, core_in, y1b, y2b, zb, za, y1a, y2a, full, mix, mix_in, mix_z, outs, tiles,
+    xo, wg, wu, wd, wgt, wut, wdt, part, core_in, y1b, y2b, zb, za, y1a, y2a, full, mix, mix_in, mix_z, outs, sums,
     send_sem, recv_sem, load_sem, weight_sem, store_sem, tile_sem, out_sem,
 ):
     row, col = lax.axis_index("row"), lax.axis_index("col")
@@ -376,22 +378,28 @@
         outs[i] = (total + mix_z[i].astype(F32)).astype(BF16)
         store(outs.at[i], (mix_out, gi_out)[i], out_sem.at[i])
 
-    done = []
-
-    def weight_tile(k):
+    begun, done = [], []
+
+    def weight_tile(k, first, end):
         tile = half // 2
         a, t = k // 4, k % 4
-        units = full[LATE:, t // 2, :, :, a, :, (low, high)[t % 2]].reshape((CHUNKS - LATE) * rows, tile)
-        side = xo[LATE:, a // 2].reshape((CHUNKS - LATE) * rows, width)
-        if k >= 2:
-            done[k - 2].wait()
-        if a == 2:
-            tiles[k % 2] = dot(units, side, TN).astype(PARTIAL)
-            dst = down_out.at[t]
-        else:
-            tiles[k % 2] = dot(side, units, TN).astype(PARTIAL)
-            dst = (gate_out, up_out)[a].at[t]
-        copy = pltpu.make_async_copy(tiles.at[k % 2], dst, tile_sem.at[k])
+        units = full[first:end, t // 2, :, :, a, :, (low, high)[t % 2]].reshape((end - first) * rows, tile)
+        side = xo[first:end, a // 2].reshape((end - first) * rows, width)
+        value = dot(units, side, TN) if a == 2 else dot(side, units, TN)
+        if first > LATE:
+            value = value + sums[a, t].astype(F32)
+        sums[a, t] = value.astype(PARTIAL)
+
+    def weight_first():
+        weight_tile(len(begun), LATE, SPLIT)
+        begun.append(True)
+
+    def weight_second():
+        k = len(done)
+        weight_tile(k, SPLIT, CHUNKS)
+        copy = pltpu.make_async_copy(
+            sums.at[k // 4, k % 4], (gate_out, up_out, down_out)[k // 4].at[k % 4], tile_sem.at[k]
+        )
         copy.start()
         done.append(copy)
 
@@ -411,7 +419,7 @@
         "ZF": far_single, "YF": far_pair, "ZA": spread_rest, "MIX": output_mixed, "GI": output_grad,
         "RS0": lambda j: row_sum(0), "RS1": lambda j: row_sum(1),
         "FI0": lambda j: finish(0), "FI1": lambda j: finish(1),
-        "W": lambda j: weight_tile(len(done)),
+        "WA": lambda j: weight_first(), "WB": lambda j: weight_second(),
     }
     sent = []
     for name, j in ORDER:
@@ -420,7 +428,7 @@
         if len(sent) > 40:
             settle(sent[-41])
     settle(len(pending))
-    for copy in stores + done[-2:]:
+    for copy in stores + done:
         copy.wait()
 
 
@@ -470,7 +478,7 @@
             buffer(CHUNKS - 2, 2, rows, width),
             buffer(2, rows, width),
             buffer(2, rows, width),
-            pltpu.VMEM((2, width, hidden // 4), PARTIAL),
+            pltpu.VMEM((3, 4, width, hidden // 4), PARTIAL),
             pltpu.SemaphoreType.DMA((COPIES,)),
             pltpu.SemaphoreType.DMA((COPIES,)),
             pltpu.SemaphoreType.DMA((2,)),

time: 124 us -> 122 us (0.984)
  Pallas kernels: 123 us -> 121 us
    pallas_call x1, Pallas kernels: 115 us -> 114 us  [exchange(): pl.pallas_call(kernel, out_shape=outputs, in_specs=[any_space] * 5, out_s...]
where the time goes in v4:
time: 122 us
  Pallas kernels  121 us (99%)
    pallas_call x1, Pallas kernels, exchange(): pl.pallas_call(kernel, out_shape=outputs, in_specs=[any_space] * 5, out_s...  114 us
    pallas_call x1, Pallas kernels, weight_grads(): pl.pallas_call(weight_kernel, out_shape=(jax.ShapeDtypeStruct(mixed.shape...  7.82 us

profile of v4, /device:TPU:1, one launch (start us, length us, event | category | flops | bytes accessed | tf_op | source)
XLA Modules:
  0.0 122.3 jit_solution(8610038433141744177)
XLA Ops:
  0.6 113.7 %shard_map.92 = (bf16[2,4,2,16,2048]{4,3,2,1,0:T(8,128)(2,1)}, bf16[2,4,2,16,2048]{4,3,2,1,0:T(8,128)(2,1)}, bf16[2,4,2,16,2048]{4,3,2,1,0:T(8,128)(2,1)}, bf16[...) custom-call(bf16[128,512]{1,0:T(8,128)(2,1)} %x_hbm.1, ...), custom_call_target="tpu_custom_call" | custom-call | tf_op jit(solution)/shard_map/pallas_call | solution.py:455
  114.3 7.8 %shard_map.93 = (bf16[128,512]{1,0:T(8,128)(2,1)}, bf16[128,512]{1,0:T(8,128)(2,1)}, f32[512,2048]{1,0:T(8,128)}, f32[512,2048]{1,0:T(8,128)}, f32[2048,512]{1,0:T(8,128)}) custom-call(bf16[256,512]{1,0:T(8,128)(2,1)} %bitcast.8, bf16[256,512]{1,0:T(8,128)(2,1)} %bitcast.9, bf16[256,2048]{1,0:T(8,128)(2,1)} %bitcast.6, bf16[256,2048]{1,0:T(8,128)(2,1)} %bitcast.7, ...), custom_call_target="tpu_custom_call" | custom-call | tf_op jit(solution)/shard_map/pallas_call | solution.py:546

commit v5 on v4

--- a/solution.py
+++ b/solution.py
@@ -32,28 +32,29 @@
 
 
 ORDER = (
-    ("R0", 0), ("R1", 0), ("G", 0), ("U", 0), ("A", 0), ("CB", 0), ("CA", 0), ("G", 1), ("U", 1), ("G", 7),
-    ("P0", 0), ("FB+", 0), ("FB-", 0), ("U", 7), ("CB", 1), ("T1", 0), ("G", 5), ("CB", 7), ("A", 1), ("G", 6),
-    ("U", 5), ("FA", 0), ("CA", 1), ("FB-", 1), ("A", 6), ("CB", 5), ("T0", 0), ("A", 5), ("CA", 6), ("FB+", 7),
-    ("FB-", 7), ("U", 6), ("P1", 0), ("CA", 5), ("G", 4), ("U", 4), ("CB", 6), ("FA", 1), ("FB+", 5), ("SA-", 0),
-    ("G", 3), ("CB", 4), ("FB-", 5), ("U", 3), ("G", 2), ("FA", 6), ("U", 2), ("SA+", 0), ("A", 4), ("FB+", 6),
-    ("A", 3), ("CB", 2), ("FA", 5), ("SA+", 1), ("FB-", 6), ("CA", 4), ("CA", 3), ("SB", 7), ("A", 2), ("SA-", 1),
-    ("FB+", 1), ("A", 7), ("FB+", 4), ("CB", 3), ("CA", 2), ("FB-", 4), ("SB", 0), ("CA", 7), ("SA+", 6), ("FA", 4),
-    ("SB", 5), ("SA-", 6), ("FB+", 2), ("FB-", 2), ("FA", 3), ("SA+", 5), ("SA-", 5), ("SB", 6), ("SB", 1),
-    ("FA", 2), ("FB-", 3), ("FB+", 3), ("SB", 4), ("SA-", 4), ("SA+", 4), ("FA", 7), ("SB", 2), ("SA+", 3),
-    ("SA-", 3), ("ACT", 5), ("SA+", 2), ("SA-", 2), ("SB", 3), ("SA+", 7), ("SA-", 7), ("ACT", 4), ("YA+", 5),
-    ("YA-", 5), ("ACT", 2), ("YA+", 4), ("ACT", 3), ("YA-", 4), ("ZB", 4), ("ZF", 5), ("YA+", 2), ("YA-", 2),
-    ("ZB", 2), ("YA-", 3), ("YA+", 3), ("ZB", 3), ("ZF", 4), ("YB+", 4), ("ZA", 5), ("YB-", 4), ("ACT", 1),
-    ("ZF", 2), ("MIX", 5), ("YB-", 2), ("YB+", 2), ("ZF", 3), ("ACT", 6), ("YB+", 3), ("YB-", 3), ("ACT", 7),
-    ("ZA", 4), ("YF", 4), ("YA+", 1), ("YA-", 1), ("MIX", 4), ("GI", 4), ("YF", 2), ("ZA", 2), ("ZB", 5),
-    ("YA+", 6), ("YA-", 6), ("GI", 2), ("ZA", 3), ("MIX", 2), ("YF", 3), ("YA+", 7), ("YA-", 7), ("ZB", 6),
-    ("MIX", 3), ("GI", 3), ("ZB", 7), ("ZF", 1), ("WA", 0), ("YB+", 5), ("YB-", 5), ("WA", 0), ("ZF", 6), ("ZF", 7),
-    ("WA", 0), ("WA", 0), ("WA", 0), ("YB+", 6), ("YB-", 6), ("WA", 0), ("WA", 0), ("WA", 0), ("WA", 0), ("YB-", 7),
-    ("YB+", 7), ("WA", 0), ("WA", 0), ("WA", 0), ("ZA", 1), ("YF", 5), ("ZB", 1), ("ACT", 0), ("YF", 6), ("MIX", 1),
-    ("RS0", 0), ("GI", 5), ("ZA", 6), ("YF", 7), ("GI", 6), ("YA-", 0), ("YB-", 1), ("YA+", 0), ("YB+", 1),
-    ("MIX", 6), ("ZA", 7), ("GI", 7), ("ZB", 0), ("MIX", 7), ("ZF", 0), ("WB", 0), ("WB", 0), ("YF", 1), ("WB", 0),
-    ("WB", 0), ("WB", 0), ("WB", 0), ("YB+", 0), ("YB-", 0), ("GI", 1), ("RS1", 0), ("WB", 0), ("WB", 0), ("ZA", 0),
-    ("WB", 0), ("WB", 0), ("WB", 0), ("YF", 0), ("MIX", 0), ("FI0", 0), ("WB", 0), ("GI", 0), ("FI1", 0),
+    ("R0", 0), ("G", 0), ("U", 0), ("CB", 0), ("R1", 0), ("A", 0), ("G", 7), ("U", 7), ("CA", 0), ("FB+", 0),
+    ("FB-", 0), ("G", 1), ("CB", 7), ("U", 1), ("P0", 0), ("G", 6), ("A", 1), ("CB", 1), ("A", 7), ("FB+", 7),
+    ("U", 6), ("CA", 7), ("A", 6), ("P1", 0), ("FB-", 7), ("SB", 0), ("CB", 6), ("FB-", 1), ("A", 5), ("CA", 1),
+    ("CA", 6), ("G", 3), ("FB+", 1), ("CA", 5), ("G", 5), ("U", 5), ("FB+", 6), ("FB-", 6), ("U", 3), ("CB", 5),
+    ("G", 4), ("G", 2), ("CB", 3), ("U", 2), ("A", 3), ("U", 4), ("T1", 0), ("A", 4), ("CA", 3), ("FA", 6),
+    ("CB", 4), ("FB-", 3), ("SB", 6), ("FA", 1), ("FB+", 3), ("FA", 5), ("CA", 4), ("CB", 2), ("A", 2), ("FA", 3),
+    ("CA", 2), ("SB", 1), ("FB+", 4), ("SB", 3), ("FB-", 4), ("FB+", 2), ("FB-", 2), ("FA", 4), ("SA+", 3),
+    ("SA+", 5), ("SA-", 3), ("FA", 2), ("SB", 7), ("SA-", 6), ("FB+", 5), ("FB-", 5), ("SB", 4), ("SB", 2),
+    ("SA-", 4), ("SA+", 4), ("ACT", 3), ("SA+", 2), ("SA-", 2), ("SB", 5), ("SA-", 1), ("YA+", 3), ("SA+", 1),
+    ("YA-", 3), ("ACT", 4), ("FA", 7), ("ACT", 2), ("ZF", 3), ("YA-", 4), ("YA+", 4), ("SA-", 5), ("ACT", 1),
+    ("SA+", 7), ("YA-", 2), ("ZF", 4), ("YA+", 2), ("ZB", 4), ("ZA", 3), ("YA+", 1), ("YA-", 1), ("ACT", 5),
+    ("MIX", 3), ("ZB", 2), ("ZF", 2), ("ZB", 3), ("YB+", 4), ("SA-", 7), ("ZF", 1), ("YA+", 5), ("ZA", 4),
+    ("SA+", 6), ("YB-", 4), ("T0", 0), ("MIX", 4), ("YA-", 5), ("YB-", 2), ("YB+", 2), ("YB+", 3), ("ZA", 2),
+    ("YB-", 3), ("ACT", 7), ("FA", 0), ("MIX", 2), ("YF", 4), ("ZF", 5), ("ACT", 6), ("ZA", 1), ("YF", 2),
+    ("GI", 4), ("YF", 3), ("MIX", 1), ("YA+", 7), ("GI", 2), ("YA-", 7), ("ZB", 5), ("GI", 3), ("YA-", 6),
+    ("ZA", 5), ("YA+", 6), ("ZB", 7), ("WA", 0), ("ZF", 7), ("MIX", 5), ("ZB", 6), ("SA-", 0), ("SA+", 0),
+    ("YB-", 5), ("YB+", 5), ("WA", 0), ("ZF", 6), ("WA", 0), ("WA", 0), ("ZB", 1), ("WA", 0), ("YB+", 7),
+    ("YB-", 7), ("WA", 0), ("WA", 0), ("YB+", 6), ("WA", 0), ("YB-", 6), ("ACT", 0), ("ZA", 7), ("WA", 0),
+    ("RS0", 0), ("YF", 5), ("WA", 0), ("MIX", 7), ("YB-", 1), ("ZA", 6), ("WA", 0), ("WA", 0), ("YF", 7), ("GI", 5),
+    ("YB+", 1), ("YF", 6), ("MIX", 6), ("YA-", 0), ("YA+", 0), ("ZB", 0), ("GI", 7), ("GI", 6), ("WB", 0),
+    ("YF", 1), ("WB", 0), ("ZF", 0), ("WB", 0), ("WB", 0), ("YB+", 0), ("YB-", 0), ("GI", 1), ("WB", 0), ("RS1", 0),
+    ("WB", 0), ("WB", 0), ("WB", 0), ("YF", 0), ("WB", 0), ("WB", 0), ("ZA", 0), ("WB", 0), ("WB", 0), ("GI", 0),
+    ("MIX", 0), ("FI0", 0), ("FI1", 0),
 )
 
 

time: 122 us -> 121 us (level)
    pallas_call x1, Pallas kernels: 114 us -> 112 us  [exchange(): pl.pallas_call(kernel, out_shape=outputs, in_specs=[any_space] * 5, out_s...]
where the time goes in v5:
time: 121 us
  Pallas kernels  120 us (99%)
    pallas_call x1, Pallas kernels, exchange(): pl.pallas_call(kernel, out_shape=outputs, in_specs=[any_space] * 5, out_s...  112 us
    pallas_call x1, Pallas kernels, weight_grads(): pl.pallas_call(weight_kernel, out_shape=(jax.ShapeDtypeStruct(mixed.shape...  7.81 us

profile of v5, /device:TPU:1, one launch (start us, length us, event | category | flops | bytes accessed | tf_op | source)
XLA Modules:
  0.0 120.6 jit_solution(6661997629091362106)
XLA Ops:
  0.6 112.0 %shard_map.92 = (bf16[2,4,2,16,2048]{4,3,2,1,0:T(8,128)(2,1)}, bf16[2,4,2,16,2048]{4,3,2,1,0:T(8,128)(2,1)}, bf16[2,4,2,16,2048]{4,3,2,1,0:T(8,128)(2,1)}, bf16[...) custom-call(bf16[128,512]{1,0:T(8,128)(2,1)} %x_hbm.1, ...), custom_call_target="tpu_custom_call" | custom-call | tf_op jit(solution)/shard_map/pallas_call | solution.py:456
  112.6 7.8 %shard_map.93 = (bf16[128,512]{1,0:T(8,128)(2,1)}, bf16[128,512]{1,0:T(8,128)(2,1)}, f32[512,2048]{1,0:T(8,128)}, f32[512,2048]{1,0:T(8,128)}, f32[2048,512]{1,0:T(8,128)}) custom-call(bf16[256,512]{1,0:T(8,128)(2,1)} %bitcast.8, bf16[256,512]{1,0:T(8,128)(2,1)} %bitcast.9, bf16[256,2048]{1,0:T(8,128)(2,1)} %bitcast.6, bf16[256,2048]{1,0:T(8,128)(2,1)} %bitcast.7, ...), custom_call_target="tpu_custom_call" | custom-call | tf_op jit(solution)/shard_map/pallas_call | solution.py:547
